TPU v7x, 128 devices: a whole 4x4x4 slice. The times are simulated.
128 devices in a mesh: slide: 8 (over x, z_hi), seq: 16 (over y, z_lo, core).
Axes of the slice: x: 4, y: 4, z: 4 (z_hi: 2, z_lo: 2; z = z_hi * 2 + z_lo), core: 2. Of those that a mesh axis runs over, the one named last changes fastest.
Arguments:
- tiles: bfloat16 [131072, 1536], P(('slide', 'seq')), may hold values from -6 to 6
- destination: int32 [131072], P(('slide', 'seq')), may hold values from 0 to 131071, as said below
- valid_len: int32 [8], replicated, may hold values from 4096 to 16384, as said below
- in_weight: bfloat16 [1536, 768], replicated, may hold values from -0.15625 to 0.15625
- norm_gain: float32 [768], replicated, may hold values from 0.25 to 1.75
- qkv_weight: bfloat16 [768, 2304], replicated, may hold values from -1 to 1
- out_weight: bfloat16 [768, 768], replicated, may hold values from -0.21875 to 0.21875
Outputs:
- encoded: bfloat16 [8, 16384, 768], P('slide', 'seq')
Inputs may be any that keep to these rules, and one draw needn't show every extreme that they name: destination is a permutation of the 131072 flat positions; the rows of device d (devices in slide-major order) form consecutive blocks of 8 rows, block j holding only positions j * 1024 to (j + 1) * 1024 - 1. `valid_len`: one slide is full and one has exactly 4096 real tiles.
All inputs are finite; a program needn't handle non-finite values.
Results may differ from a plain program's by a relative error of at most 0.012.
Values may be sent and summed in bfloat16 or wider, within the bound.
A program may use at most 256 MiB of HBM per device.

v0:
```python
import jax
import jax.numpy as jnp
from jax import lax
from jax.sharding import PartitionSpec as P

HEAD_COUNT = 12
FIRST_SEGMENT = 8192
SECOND_SEGMENT = 32768
THIRD_SEGMENT = 65536
FIRST_DILATION = 4
SECOND_DILATION = 8
THIRD_DILATION = 16


def pick_rows(input_matrix, row_total, period, head_total, head_width, offsets):
    reshaped_input = input_matrix.reshape(row_total, period, head_total, head_width)
    picker = (jnp.arange(period, dtype=jnp.int32)[:, None] == offsets[None, :]).astype(
        input_matrix.dtype
    )
    picked = jnp.sum(reshaped_input * picker[None, :, :, None], axis=1, dtype=input_matrix.dtype)
    return picked.reshape(row_total, head_total * head_width)


def select_heads(input_matrix, row_total, dilation_rate, head_total, head_width):
    offsets = jnp.arange(head_total, dtype=jnp.int32) % dilation_rate
    return pick_rows(input_matrix, row_total, dilation_rate, head_total, head_width, offsets)


def scatter_back(value_input, row_total, dilation_rate, head_total, fill_value):
    selected_rows = (
        jnp.arange(dilation_rate, dtype=jnp.int32)[:, None]
        == (jnp.arange(head_total, dtype=jnp.int32) % dilation_rate)[None, :]
    )
    if value_input.ndim == 2:
        return jnp.where(selected_rows[None], value_input[:, None, :], fill_value).reshape(
            row_total * dilation_rate, head_total
        )
    return jnp.where(selected_rows[None, :, :, None], value_input[:, None], fill_value).reshape(
        row_total * dilation_rate, head_total, value_input.shape[-1]
    )


def local(tiles, destination, valid_len, in_weight, norm_gain, qkv_weight, out_weight):
    tiles_per_device = tiles.shape[0]
    width = in_weight.shape[1]
    head_total = HEAD_COUNT
    head_width = width // head_total
    n_seq = lax.axis_size("seq")
    length = tiles_per_device * n_seq
    proj = jnp.dot(tiles, in_weight, preferred_element_type=jnp.float32).astype(jnp.bfloat16)
    local_pos = destination % tiles_per_device
    id_parts = jnp.stack([local_pos // 128, local_pos % 128], axis=1).astype(jnp.bfloat16)
    moved, moved_ids = (
        lax.all_to_all(proj, ("slide", "seq"), split_axis=0, concat_axis=0, tiled=True),
        lax.all_to_all(id_parts, ("slide", "seq"), split_axis=0, concat_axis=0, tiled=True),
    )
    place = (
        moved_ids[:, 0].astype(jnp.float32) * 128.0 + moved_ids[:, 1].astype(jnp.float32)
    ).astype(jnp.int32)
    emb = jnp.zeros((tiles_per_device, width), jnp.bfloat16).at[place].set(moved)
    value_input = emb.astype(jnp.float32)
    mean = jnp.mean(value_input, axis=-1, keepdims=True)
    var = jnp.mean((value_input - mean) ** 2, axis=-1, keepdims=True)
    normed = ((value_input - mean) * lax.rsqrt(var + 1e-05) * norm_gain).astype(jnp.bfloat16)
    qkv = jnp.dot(normed, qkv_weight, preferred_element_type=jnp.float32).astype(jnp.bfloat16)
    query_input = qkv[:, :width]
    key_segments = qkv[:, width : 2 * width]
    value_segments = qkv[:, 2 * width :]
    slide_index = lax.axis_index("slide")
    seq_index = lax.axis_index("seq")
    slide_rows = jnp.arange(valid_len.shape[0], dtype=jnp.int32)
    valid_length = jnp.sum(jnp.where(slide_rows == slide_index, valid_len, 0))
    scale = 1.0 / head_width**0.5
    head_numbers = jnp.arange(head_total, dtype=jnp.int32)
    branch_result = []
    for segment_length, dilation_rate in (
        (FIRST_SEGMENT, FIRST_DILATION),
        (SECOND_SEGMENT, SECOND_DILATION),
        (THIRD_SEGMENT, THIRD_DILATION),
    ):
        segment_span = min(segment_length, length)
        head_group = segment_span // tiles_per_device
        row_total = tiles_per_device // dilation_rate
        key_total = head_group * row_total
        query_rows = select_heads(query_input, row_total, dilation_rate, head_total, head_width)
        start = seq_index // head_group * head_group * row_total
        key_rows = select_heads(key_segments, row_total, dilation_rate, head_total, head_width)
        value_rows = select_heads(value_segments, row_total, dilation_rate, head_total, head_width)
        all_keys, all_values = (
            lax.all_gather(key_rows, "seq", axis=0, tiled=True),
            lax.all_gather(value_rows, "seq", axis=0, tiled=True),
        )
        seg_keys = lax.dynamic_slice_in_dim(all_keys, start, key_total, 0)
        seg_values = lax.dynamic_slice_in_dim(all_values, start, key_total, 0)
        group_offset = seq_index // head_group * head_group * tiles_per_device
        query_heads = query_rows.reshape(row_total, head_total, head_width)
        key_heads = seg_keys.reshape(key_total, head_total, head_width)
        value_heads = seg_values.reshape(key_total, head_total, head_width)
        key_position = (
            group_offset
            + jnp.arange(key_total, dtype=jnp.int32)[None, :] * dilation_rate
            + (head_numbers % dilation_rate)[:, None]
        )
        scores = (
            jnp.einsum("qhd,khd->hqk", query_heads, key_heads, preferred_element_type=jnp.float32)
            * scale
        )
        scores = jnp.where((key_position < valid_length)[:, None, :], scores, -1e30)
        top = jnp.max(scores, axis=-1)
        expo = jnp.exp(scores - top[..., None])
        total = jnp.sum(expo, axis=-1)
        numer = jnp.einsum(
            "hqk,khd->qhd",
            expo.astype(jnp.bfloat16),
            value_heads,
            preferred_element_type=jnp.float32,
        )
        branch_result.append(
            (
                scatter_back(top.T, row_total, dilation_rate, head_total, -1e30),
                scatter_back(total.T, row_total, dilation_rate, head_total, 0.0),
                scatter_back(numer, row_total, dilation_rate, head_total, 0.0),
            )
        )
    upper = jnp.maximum(jnp.maximum(branch_result[0][0], branch_result[1][0]), branch_result[2][0])
    denom = jnp.zeros((tiles_per_device, head_total), jnp.float32)
    numer_sum = jnp.zeros((tiles_per_device, head_total, head_width), jnp.float32)
    for top, total, part in branch_result:
        factor = jnp.exp(top - upper)
        denom = denom + factor * total
        numer_sum = numer_sum + factor[..., None] * part
    query_position = seq_index * tiles_per_device + jnp.arange(tiles_per_device, dtype=jnp.int32)
    covered_rows = (
        query_position[:, None] % FIRST_DILATION == head_numbers[None, :] % FIRST_DILATION
    ) & (query_position[:, None] < valid_length)
    safe = jnp.where(covered_rows, denom, 1.0)
    attn = (
        jnp.where(covered_rows[..., None], numer_sum / safe[..., None], 0.0)
        .reshape(tiles_per_device, width)
        .astype(jnp.bfloat16)
    )
    encoded = jnp.dot(attn, out_weight, preferred_element_type=jnp.float32).astype(jnp.bfloat16)
    return encoded.reshape(1, tiles_per_device, width)


def solution(mesh):
    in_specs = (P(("slide", "seq"), None), P(("slide", "seq")), P(), P(), P(), P(), P())
    out_specs = P("slide", "seq", None)
    return jax.shard_map(local, mesh=mesh, in_specs=in_specs, out_specs=out_specs, check_vma=False)
```

profile of v0, /device:TPU:1, one launch (start us, length us, event | category | flops | bytes accessed | tf_op | source)
XLA Modules:
  0.0 429.8 jit_solution(13476885775567768077)
XLA Ops:
  10.3 12.0 %all-to-all-start = ((bf16[128,8,2]{1,2,0:T(2,128)(2,1)}), bf16[128,8,2]{1,2,0:T(2,128)(2,1)}, u32[]{:S(2)}, u32[]{:S(2)}) async-start(bf16[128,8,2]{1,2,0:T(2,128)(2,1)} %copy.155), calls=%async_computation | async-start | bytes 131072 | tf_op jit(solution)/shard_map/all_to_all | solution.py:55
  22.3 6.4 %fusion.37 = bf16[128,8,768]{2,1,0:T(8,128)(2,1)} fusion(bf16[1024,1536]{1,0:T(8,128)(2,1)} %param.7, bf16[1536,768]{1,0:T(8,128)(2,1)} %param.10), kind=kOutput, calls=%fused_computation.58 | convolution fusion | flops 2416705536 | bytes 7077888 | tf_op jit(solution)/shard_map/dot_general | solution.py:50
  32.1 6.7 %all-to-all-start.1 = ((bf16[128,8,768]{2,1,0:T(8,128)(2,1)}), bf16[128,8,768]{2,1,0:T(8,128)(2,1)}, u32[]{:S(2)}, u32[]{:S(2)}) async-start(bf16[128,8,768]{2,1,0:T(8,128)(2,1)} %fusion.37), calls=%async_computation.1 | async-start | bytes 3145728 | tf_op jit(solution)/shard_map/all_to_all | solution.py:54
  42.4 20.6 %all-to-all-done.1 = bf16[128,8,768]{2,1,0:T(8,128)(2,1)} async-done(((bf16[128,8,768]{2,1,0:T(8,128)(2,1)}), bf16[128,8,768]{2,1,0:T(8,128)(2,1)}, u32[]{:S(2)}, u32[]{:S(2)}) %all-to-all-start.1) | async-done | bytes 1572896 | tf_op jit(solution)/shard_map/all_to_all | solution.py:54
  63.1 7.2 %scatter_custom_fusion = bf16[1024,768]{1,0:T(8,128)(2,1)} fusion(s32[1024]{0:T(1024)S(1)} %bitcast.107, bf16[128,8,768]{2,1,0:T(8,128)(2,1)} %all-to-all-done.1, bf16[]{:T(256)} %constant.211.clone.1), kind=kCustom, calls=%fused_computation.48 | custom fusion | bytes 3145730 | tf_op jit(solution)/shard_map/scatter | solution.py:60
  80.0 5.9 %reshape.730 = bf16[64,16,12,64]{3,2,1,0:T(8,128)(2,1)} reshape(bf16[1024,768]{1,0:T(8,128)(2,1)} %get-tuple-element.18) | data formatting | bytes 3145728 | tf_op jit(solution)/shard_map/reshape | solution.py:16
  93.6 10.0 %multiply_reduce_fusion.4 = (bf16[64,12,64]{2,1,0:T(8,128)(2,1)}, bf16[64,12,64]{2,1,0:T(8,128)(2,1)}, bf16[64,12,64]{2,1,0:T(8,128)(2,1)S(1)}) fusion(bf16[64,16,12,64]{3,2,1,0:T(8,128)(2,1)} %reshape.720, bf16[16,12]{1,0:T(8,128)(2,1)S(1)} %get-tuple-element.28, bf16[64,16,12,64]{3,2,1,0:T(8,128)(2,1)} %reshape.721, bf16[64,16,12,64]{3,2,1,0:T(8,128)(2,1)} %reshape.730), kind=kLoop, calls=%fused_computation.20 | loop fusion | flops 4571136 | bytes 5013888 | tf_op jit(solution)/shard_map/reduce_sum | solution.py:20
  106.6 6.0 %reshape.727 = bf16[128,8,12,64]{3,2,1,0:T(8,128)(2,1)} reshape(bf16[1024,768]{1,0:T(8,128)(2,1)} %get-tuple-element.18) | data formatting | bytes 3145728 | tf_op jit(solution)/shard_map/reshape | solution.py:16
  120.3 9.5 %multiply_reduce_fusion.6 = (bf16[128,12,64]{2,1,0:T(8,128)(2,1)}, bf16[128,12,64]{2,1,0:T(8,128)(2,1)}, bf16[128,12,64]{2,1,0:T(8,128)(2,1)}) fusion(bf16[128,8,12,64]{3,2,1,0:T(8,128)(2,1)} %reshape.716, bf16[8,12]{1,0:T(8,128)(2,1)S(1)} %get-tuple-element.26, bf16[128,8,12,64]{3,2,1,0:T(8,128)(2,1)} %reshape.717, bf16[128,8,12,64]{3,2,1,0:T(8,128)(2,1)} %reshape.727), kind=kLoop, calls=%fused_computation.22 | loop fusion | flops 4423680 | bytes 5308608 | tf_op jit(solution)/shard_map/reduce_sum | solution.py:20
  134.1 6.0 %reshape.724 = bf16[256,4,12,64]{3,2,1,0:T(8,128)(2,1)} reshape(bf16[1024,768]{1,0:T(8,128)(2,1)} %get-tuple-element.18) | data formatting | bytes 3145728 | tf_op jit(solution)/shard_map/reshape | solution.py:16
  147.8 9.8 %multiply_reduce_fusion.8 = (bf16[256,12,64]{2,1,0:T(8,128)(2,1)}, bf16[256,12,64]{2,1,0:T(8,128)(2,1)S(1)}, bf16[256,12,64]{2,1,0:T(8,128)(2,1)S(1)}) fusion(bf16[256,4,12,64]{3,2,1,0:T(8,128)(2,1)} %reshape.712, bf16[4,12]{1,0:T(4,128)(2,1)S(1)} %get-tuple-element.24, bf16[256,4,12,64]{3,2,1,0:T(8,128)(2,1)} %reshape.713, bf16[256,4,12,64]{3,2,1,0:T(8,128)(2,1)} %reshape.724), kind=kLoop, calls=%fused_computation.24 | loop fusion | flops 4128768 | bytes 5898336 | tf_op jit(solution)/shard_map/reduce_sum | solution.py:20
  188.5 5.7 %broadcast_in_dim.376 = f32[1024,768]{1,0:T(8,128)S(1)} reshape(f32[64,16,12,64]{3,2,1,0:T(8,128)} %broadcast_in_dim.375) | data formatting | bytes 6291456 | tf_op jit(solution)/shard_map/jit(_where)/broadcast_in_dim | solution.py:38
  196.5 16.3 %all-gather.9.cloned.1.call-done = bf16[2048,768]{0,1:T(8,128)(2,1)} async-done(((bf16[128,768]{0,1:T(8,128)(2,1)}), bf16[2048,768]{0,1:T(8,128)(2,1)}) %all-gather.9.cloned.1.call-update) | async-done | bytes 3145744 | tf_op jit(solution)/shard_map/all_gather | solution.py:90
  212.9 8.6 %fusion.6 = (f32[12,128]{1,0:T(8,128)S(1)}, f32[12,128,2048]{2,1,0:T(8,128)}) fusion(pred[12,2048]{1,0:T(8,128)(4,1)S(1)} %copy-done.7, bf16[2048,12,64]{0,2,1:T(8,128)(2,1)} %bitcast.91, bf16[128,12,64]{2,1,0:T(8,128)(2,1)} %get-tuple-element.8), kind=kOutput, calls=%fused_computation.10 | convolution fusion | flops 412088832 | bytes 15955968 | tf_op jit(solution)/shard_map/qhd,khd->hqk/dot_general | solution.py:105
  221.5 34.4 %all-gather.15.cloned.1.call-done = bf16[2048,768]{0,1:T(8,128)(2,1)} async-done(((bf16[128,768]{0,1:T(8,128)(2,1)}), bf16[2048,768]{0,1:T(8,128)(2,1)}) %all-gather.15.cloned.1.call-update) | async-done | bytes 3145744 | tf_op jit(solution)/shard_map/all_gather | solution.py:91
  255.9 8.4 %fusion.44 = f32[128,12,64]{0,2,1:T(8,128)S(1)} fusion(bf16[2048,12,64]{0,2,1:T(8,128)(2,1)} %bitcast.108, f32[12,128,2048]{2,1,0:T(8,128)} %get-tuple-element.32, f32[12,128]{1,0:T(8,128)S(1)} %get-tuple-element.31, pred[12,2048]{1,0:T(8,128)(4,1)S(1)} %copy-done.7), kind=kOutput, calls=%fused_computation.61 | convolution fusion | flops 415236096 | bytes 16152576 | tf_op jit(solution)/shard_map/hqk,khd->qhd/dot_general | solution.py:112
  265.4 6.8 %fusion.7 = f32[12,128]{1,0:T(8,128)S(1)} fusion(f32[12,128,2048]{2,1,0:T(8,128)} %get-tuple-element.32, f32[12,128]{1,0:T(8,128)S(1)} %get-tuple-element.31, pred[12,2048]{1,0:T(8,128)(4,1)S(1)} %copy-done.7), kind=kLoop, calls=%fused_computation.11 | loop fusion | flops 12581376 | bytes 12619776 | tf_op jit(solution)/shard_map/reduce_sum | solution.py:111
  276.8 5.7 %broadcast_in_dim.372 = f32[1024,768]{1,0:T(8,128)S(1)} reshape(f32[128,8,12,64]{3,2,1,0:T(8,128)} %broadcast_in_dim.371) | data formatting | bytes 6291456 | tf_op jit(solution)/shard_map/jit(_where)/broadcast_in_dim | solution.py:38
  285.0 24.8 %all-gather.7.cloned.1.call-done = bf16[4096,768]{0,1:T(8,128)(2,1)} async-done(((bf16[256,768]{0,1:T(8,128)(2,1)}), bf16[4096,768]{0,1:T(8,128)(2,1)}) %all-gather.7.cloned.1.call-update) | async-done | bytes 6291472 | tf_op jit(solution)/shard_map/all_gather | solution.py:90
  309.8 53.9 %all-gather.13.cloned.1.call-done = bf16[4096,768]{0,1:T(8,128)(2,1)} async-done(((bf16[256,768]{0,1:T(8,128)(2,1)}), bf16[4096,768]{0,1:T(8,128)(2,1)}) %all-gather.13.cloned.1.call-update) | async-done | bytes 6291472 | tf_op jit(solution)/shard_map/all_gather | solution.py:91
  367.6 10.2 %fusion = (f32[12,256]{1,0:T(8,128)S(1)}, f32[12,256,2048]{2,1,0:T(8,128)}) fusion(pred[12,2048]{1,0:T(8,128)(4,1)S(1)} %copy-done.5, bf16[2048,12,64]{0,2,1:T(8,128)(2,1)S(1)} %bitcast.89, bf16[256,12,64]{2,1,0:T(8,128)(2,1)S(1)} %copy-done.3), kind=kOutput, calls=%fused_computation.3 | convolution fusion | flops 824177664 | bytes 28741632 | tf_op jit(solution)/shard_map/qhd,khd->hqk/dot_general | solution.py:105
  377.7 11.1 %fusion.1 = f32[12,256]{1,0:T(8,128)S(1)} fusion(f32[12,256,2048]{2,1,0:T(8,128)} %get-tuple-element.34, f32[12,256]{1,0:T(8,128)S(1)} %get-tuple-element.33, pred[12,2048]{1,0:T(8,128)(4,1)S(1)} %copy-done.5), kind=kLoop, calls=%fused_computation.4 | loop fusion | flops 25162752 | bytes 25214976 | tf_op jit(solution)/shard_map/reduce_sum | solution.py:111
  388.9 10.6 %fusion.38 = f32[256,12,64]{0,2,1:T(8,128)S(1)} fusion(bf16[2048,12,64]{0,2,1:T(8,128)(2,1)S(1)} %bitcast.92, f32[12,256,2048]{2,1,0:T(8,128)} %get-tuple-element.34, f32[12,256]{1,0:T(8,128)S(1)} %get-tuple-element.33, pred[12,2048]{1,0:T(8,128)(4,1)S(1)} %copy-done.5), kind=kOutput, calls=%fused_computation.59 | convolution fusion | flops 830472192 | bytes 29134848 | tf_op jit(solution)/shard_map/hqk,khd->qhd/dot_general | solution.py:112
  405.5 5.7 %broadcast_in_dim.367 = f32[1024,768]{1,0:T(8,128)S(1)} reshape(f32[256,4,12,64]{3,2,1,0:T(8,128)} %broadcast_in_dim.366) | data formatting | bytes 6291456 | tf_op jit(solution)/shard_map/jit(_where)/broadcast_in_dim | solution.py:38
  (136 shorter events, 113.4 us)
Async XLA Ops:
  6.5 67.6 %copy-start = (bf16[768,2304]{1,0:T(8,128)(2,1)S(1)}, bf16[768,2304]{1,0:T(8,128)(2,1)}, u32[]{:S(2)}) copy-start(bf16[768,2304]{1,0:T(8,128)(2,1)} %param.12) | copy-start | bytes 10616836
  10.3 21.8 %all-to-all-start = ((bf16[128,8,2]{1,2,0:T(2,128)(2,1)}), bf16[128,8,2]{1,2,0:T(2,128)(2,1)}, u32[]{:S(2)}, u32[]{:S(2)}) async-start(bf16[128,8,2]{1,2,0:T(2,128)(2,1)} %copy.155), calls=%async_computation | async-start | bytes 131072 | tf_op jit(solution)/shard_map/all_to_all | solution.py:55
  32.1 31.0 %all-to-all-start.1 = ((bf16[128,8,768]{2,1,0:T(8,128)(2,1)}), bf16[128,8,768]{2,1,0:T(8,128)(2,1)}, u32[]{:S(2)}, u32[]{:S(2)}) async-start(bf16[128,8,768]{2,1,0:T(8,128)(2,1)} %fusion.37), calls=%async_computation.1 | async-start | bytes 3145728 | tf_op jit(solution)/shard_map/all_to_all | solution.py:54
  38.8 130.5 %all-gather.11.cloned.1.call-start = ((), (), s32[]{:S(2)}) async-start(), calls=%async_computation.4 | async-start | bytes 1671168 | tf_op jit(solution)/shard_map/all_gather | solution.py:90
  63.1 11.0 %copy-start.18 = (f32[768]{0:T(1024)S(1)}, f32[768]{0:T(1024)}, u32[]{:S(2)}) copy-start(f32[768]{0:T(1024)} %param.11) | copy-start | bytes 9220
  70.2 3.9 copy-start.2
  93.6 13.0 %copy-start.14 = (s32[12]{0:T(128)S(1)}, s32[12]{0:T(128)}, u32[]{:S(2)}) copy-start(s32[12]{0:T(128)} %get-tuple-element.36) | copy-start | bytes 148
  105.5 66.9 %all-gather.17.cloned.1.call-start = ((), (), s32[]{:S(2)}) async-start(), calls=%async_computation.7 | async-start | bytes 1671168 | tf_op jit(solution)/shard_map/all_gather | solution.py:91
  106.4 106.5 %all-gather.9.cloned.1.call-start = ((), (), s32[]{:S(2)}) async-start(), calls=%async_computation.3 | async-start | bytes 3342336 | tf_op jit(solution)/shard_map/all_gather | solution.py:90
  131.9 123.9 %all-gather.15.cloned.1.call-start = ((), (), s32[]{:S(2)}) async-start(), calls=%async_computation.6 | async-start | bytes 3342336 | tf_op jit(solution)/shard_map/all_gather | solution.py:91
  134.1 175.7 %all-gather.7.cloned.1.call-start = ((), (), s32[]{:S(2)}) async-start(), calls=%async_computation.2 | async-start | bytes 6684672 | tf_op jit(solution)/shard_map/all_gather | solution.py:90
  134.1 33.8 %copy-start.13 = (s32[12]{0:T(128)}, s32[12]{0:T(128)S(1)}, u32[]{:S(2)}) copy-start(s32[12]{0:T(128)S(1)} %and_select_fusion.2) | copy-start | bytes 148
  157.6 6.2 %copy-start.19 = (s32[8]{0:T(128)S(1)}, s32[8]{0:T(128)}, u32[]{:S(2)}) copy-start(s32[8]{0:T(128)} %param.9) | copy-start | bytes 100
  157.6 7.6 %copy-start.16 = (s32[12]{0:T(128)S(1)}, s32[12]{0:T(128)}, u32[]{:S(2)}) copy-start(s32[12]{0:T(128)} %copy-done.15) | copy-start | bytes 148
  159.1 204.6 %all-gather.13.cloned.1.call-start = ((), (), s32[]{:S(2)}) async-start(), calls=%async_computation.5 | async-start | bytes 6684672 | tf_op jit(solution)/shard_map/all_gather | solution.py:91
  165.1 9.8 %copy-start.12 = (pred[1024]{0:T(1024)(128)(4,1)}, pred[1024]{0:T(1024)(128)(4,1)S(1)}, u32[]{:S(2)}) copy-start(pred[1024]{0:T(1024)(128)(4,1)S(1)} %fusion.61) | copy-start | bytes 3076
  165.1 9.8 %copy-start.11 = (s32[1024]{0:T(1024)}, s32[1024]{0:T(1024)S(1)}, u32[]{:S(2)}) copy-start(s32[1024]{0:T(1024)S(1)} %add_select_fusion.4) | copy-start | bytes 12292
  169.3 5.6 %copy-start.6 = (bf16[64,12,64]{2,1,0:T(8,128)(2,1)S(1)}, bf16[64,12,64]{2,1,0:T(8,128)(2,1)}, u32[]{:S(2)}) copy-start(bf16[64,12,64]{2,1,0:T(8,128)(2,1)} %get-tuple-element.5) | copy-start | bytes 294916
  174.9 2.9 copy-start.4
  194.2 18.7 %copy-start.7 = (pred[12,2048]{1,0:T(8,128)(4,1)S(1)}, pred[12,2048]{1,0:T(8,128)(4,1)}, u32[]{:S(2)}) copy-start(pred[12,2048]{1,0:T(8,128)(4,1)} %add_compare_fusion) | copy-start | bytes 73732
  285.0 82.6 %copy-start.5 = (pred[12,2048]{1,0:T(8,128)(4,1)S(1)}, pred[12,2048]{1,0:T(8,128)(4,1)}, u32[]{:S(2)}) copy-start(pred[12,2048]{1,0:T(8,128)(4,1)} %add_compare_fusion.1) | copy-start | bytes 73732
  363.7 3.9 copy-start.3
  414.7 5.4 %copy-start.17 = (bf16[768,768]{1,0:T(8,128)(2,1)S(1)}, bf16[768,768]{1,0:T(8,128)(2,1)}, u32[]{:S(2)}) copy-start(bf16[768,768]{1,0:T(8,128)(2,1)} %param.13) | copy-start | bytes 3538948
  414.7 8.0 %copy-start.1 = (bf16[768,2304]{1,0:T(8,128)(2,1)S(1)}, bf16[768,2304]{1,0:T(8,128)(2,1)}, u32[]{:S(2)}) copy-start(bf16[768,2304]{1,0:T(8,128)(2,1)} %param.12) | copy-start | bytes 10616836
  (4 other events, 6.5 us)
Sparse Core Ops, SparseCore 0:
  105.6 29.4 all-gather.10
  136.8 33.2 all-gather.16
  171.7 41.1 all-gather.8
  214.4 41.4 all-gather.14
  257.3 52.4 all-gather.6
  311.3 52.3 all-gather.12
where the time goes:
time: 436 us; the launch traced here: 430 us
  waiting for transfers between devices  154 us (35%)
  local copies, waits for them, and re-layouts  122 us (28%)
  other arithmetic  66.5 us (15%)
  matrix products  54.4 us (12%)
  starting transfers between devices  19.1 us (4%)
  between operations  14.2 us (3%)
    all_gather x3, waiting for transfers between devices, local(): lax.all_gather(value_rows, 'seq', axis=0, tiled=True)  88.3 us
    all_gather x3, waiting for transfers between devices, local(): lax.all_gather(key_rows, 'seq', axis=0, tiled=True)  41.1 us
    reshape x9, local copies, waits for them, and re-layouts, pick_rows(): input_matrix.reshape(row_total, period, head_total, head_width)  41 us
    broadcast_in_dim x9, local copies, waits for them, and re-layouts, scatter_back(): jnp.where(selected_rows[None, :, :, None], value_input[:, None], fill_value)  37.2 us
    reduce_sum x3, other arithmetic, pick_rows(): jnp.sum(reshaped_input * picker[None, :, :, None], axis=1, dtype=input_ma...  29.3 us
    dot_general x3, matrix products, local(): jnp.einsum('qhd,khd->hqk', query_heads, key_heads, preferred_element_type...  21 us
    all_to_all x1, waiting for transfers between devices, local(): lax.all_to_all(proj, ('slide', 'seq'), split_axis=0, concat_axis=0, tiled...  20.6 us
    dot_general x3, matrix products, local(): jnp.einsum('hqk,khd->qhd', expo.astype(jnp.bfloat16), value_heads, prefer...  20.1 us
  transfers between devices with their start and end apart: 8, of which 6 were waited for; matrix products, arithmetic and copies ran while one was open for 32% of the time, Pallas kernels for 0%

commit v1 on v0

v1 whole, which is shorter than its diff:
```python
import functools

import jax
import jax.numpy as jnp
from jax import lax
from jax.experimental import pallas as pl
from jax.experimental.pallas import tpu as pltpu
from jax.sharding import PartitionSpec as P

MESH = pl.DeviceIdType.MESH
SLIDES = 8
SEQ = 16
DEVICES = 128
ROWS = 1024
BLOCK = 8
E = 1536
D = 768
WIDE = 640
CHUNK = 256
BF = jnp.bfloat16
F32 = jnp.float32
I32 = jnp.int32


def iota(shape, dim):
    return lax.broadcasted_iota(I32, shape, dim)


def pick_columns(qkv, place):
    rows = qkv.shape[0]
    lane = iota((rows, 128), 1)
    cls = place & 3
    high = cls >= 2
    odd = (cls & 1) == 1
    low_lane = lane < 64

    def head(kind, group):
        at = kind * D + group * 256
        return jnp.where(high, qkv[:, at + 128 : at + 256], qkv[:, at : at + 128])

    def pair(left, right):
        moved = pltpu.roll(jnp.where(odd, left, right), 64, 1)
        return jnp.where(low_lane == odd, moved, jnp.where(odd, right, left))

    step = (place >> 2) & 3
    sorted_at = cls * 256 + (((step & 1) << 1) | (step >> 1)) * 64 + (place >> 4)
    ids = jnp.where(lane == 64, sorted_at >> 7, jnp.where(lane == 65, sorted_at & 127, 0)).astype(F32)
    q2 = head(0, 2) * 0.125
    q2 = jnp.where(odd, pltpu.roll(q2, 64, 1), q2)
    return (
        pair(head(0, 0) * 0.125, head(0, 1) * 0.125),
        jnp.where(low_lane, q2, ids),
        pair(head(1, 0), head(2, 0)),
        pair(head(1, 2), head(2, 2)),
        pair(head(1, 1), head(2, 1)),
    )


def project_kernel(tiles, dest, w_in, gain, w_qkv, recv, tiles_v, w_in_v, w_qkv_v, send, load_sem, send_sem, recv_sem, own_sem):
    slide = lax.axis_index("slide")
    seq = lax.axis_index("seq")
    me = slide * SEQ + seq
    chunks = ROWS // CHUNK
    per = CHUNK // BLOCK

    def chunk_at(step):
        return lax.rem(slide // 2 + step, chunks)

    loads = [pltpu.make_async_copy(w_in, w_in_v, load_sem.at[0]), pltpu.make_async_copy(w_qkv, w_qkv_v, load_sem.at[1])]
    for step in range(chunks):
        loads.append(
            pltpu.make_async_copy(
                tiles.at[pl.ds(pl.multiple_of(chunk_at(step) * CHUNK, CHUNK), CHUNK)],
                tiles_v.at[step],
                load_sem.at[2 + step],
            )
        )
    for index in (0, 2, 1, 3, 4, 5):
        loads[index].start()

    barrier = pltpu.get_barrier_semaphore()

    @pl.loop(1, DEVICES)
    def _(i):
        other = lax.rem(me + i, DEVICES)
        pl.semaphore_signal(barrier, inc=1, device_id=(other // SEQ, lax.rem(other, SEQ)), device_id_type=MESH)

    for step in range(chunks):
        chunk = chunk_at(step)
        if step == 0:
            loads[0].wait()
        loads[2 + step].wait()
        proj = jnp.dot(tiles_v[step], w_in_v[...], preferred_element_type=F32).astype(BF).astype(F32)
        mean = jnp.mean(proj, axis=-1, keepdims=True)
        centred = proj - mean
        var = jnp.mean(centred * centred, axis=-1, keepdims=True)
        normed = (centred * lax.rsqrt(var + 1e-05) * gain[...]).astype(BF)
        if step == 0:
            loads[1].wait()
        qkv = jnp.dot(normed, w_qkv_v[...], preferred_element_type=F32)
        eye = iota((128, 128), 0) == iota((128, 128), 1)
        places = []
        for part in range(CHUNK // 128):
            line = dest[pl.ds(chunk * (CHUNK // 128) + part, 1), :] & (ROWS - 1)
            places.append(jnp.sum(jnp.where(eye, line.astype(F32), 0.0), axis=1, keepdims=True))
        place = jnp.concatenate(places, axis=0).astype(I32)
        for index, block in enumerate(pick_columns(qkv, place)):
            send[pl.ds(chunk * per, per), :, index * 128 : (index + 1) * 128] = block.reshape(per, BLOCK, 128).astype(BF)
        if step == 0:
            pl.semaphore_wait(barrier, DEVICES - 1)

        @pl.loop(0, per)
        def _(i):
            other = chunk * per + lax.rem(seq * 2 + i, per)

            @pl.when(other != me)
            def _():
                pltpu.make_async_remote_copy(
                    src_ref=send.at[other],
                    dst_ref=recv.at[me],
                    send_sem=send_sem,
                    recv_sem=recv_sem,
                    device_id=(other // SEQ, lax.rem(other, SEQ)),
                    device_id_type=MESH,
                ).start()

    own = pltpu.make_async_copy(send.at[me], recv.at[me], own_sem)
    own.start()
    own.wait()
    rest = pl.ds(0, DEVICES - 1)
    pltpu.make_async_copy(send.at[rest], send.at[rest], send_sem).wait()
    pltpu.make_async_copy(recv.at[rest], recv.at[rest], recv_sem).wait()


def project(tiles, dest, w_in, gain, w_qkv):
    anywhere = pl.BlockSpec(memory_space=pl.ANY)
    vmem = pl.BlockSpec(memory_space=pltpu.VMEM)
    return pl.pallas_call(
        project_kernel,
        out_shape=jax.ShapeDtypeStruct((DEVICES, BLOCK, WIDE), BF),
        in_specs=[anywhere, vmem, anywhere, vmem, anywhere],
        out_specs=anywhere,
        scratch_shapes=[
            pltpu.VMEM((ROWS // CHUNK, CHUNK, E), BF),
            pltpu.VMEM((E, D), BF),
            pltpu.VMEM((D, 3 * D), BF),
            pltpu.VMEM((DEVICES, BLOCK, WIDE), BF),
            pltpu.SemaphoreType.DMA((2 + ROWS // CHUNK,)),
            pltpu.SemaphoreType.DMA,
            pltpu.SemaphoreType.DMA,
            pltpu.SemaphoreType.DMA,
        ],
        compiler_params=pltpu.CompilerParams(collective_id=0, has_side_effects=True, vmem_limit_bytes=48 * 1024 * 1024),
        name="project_send",
    )(tiles, dest, w_in, gain, w_qkv)


def attend_kernel(
    recv, valid, back, own, sib, x_own, x_sib, stage, q_op, k_op, v_op, result, attn,
    send_sem, recv_sem, sib_send, sib_recv, x_send, x_recv, xs_send, xs_recv, out_send, out_recv, own_sem,
):
    slide = lax.axis_index("slide")
    seq = lax.axis_index("seq")
    half = seq // 8
    row = lax.rem(seq // 4, 2)
    col = lax.rem(seq // 2, 2)
    core = lax.rem(seq, 2)

    def chip(d):
        return lax.rem(row + d // 2, 2), lax.rem(col + d % 2, 2)

    def slot(d):
        r, c = chip(d)
        return 2 * r + c

    def cls_of(d):
        r, c = chip(d)
        return 2 * lax.rem(r + half, 2) + c

    def device(d):
        return (slide, half * 8 + slot(d) * 2 + core)

    sibling = (slide, seq + 1 - 2 * core)
    cross = (slide, (1 - half) * 8 + (2 * (1 - row) + col) * 2 + core)
    partners = [device(1), device(2), device(3), sibling, cross]

    def cross_slot(d):
        return 2 * lax.rem(1 - row + d // 2, 2) + lax.rem(col + d % 2, 2)

    barrier = pltpu.get_barrier_semaphore()
    for other in partners:
        pl.semaphore_signal(barrier, inc=1, device_id=other, device_id_type=MESH)

    rows_in = recv[...]
    lane8 = iota((8, 128), 1)
    weigh = jnp.where(lane8 == 64, 128.0, jnp.where(lane8 == 65, 1.0, 0.0)).astype(BF)
    at = lax.dot_general(weigh, rows_in[:, 128:256], (((1,), (1,)), ((), ())), preferred_element_type=F32)
    at = at[0:1].astype(I32)

    def sort_class(cls):
        hit = (at - cls * 256) == iota((256, ROWS), 0)
        one_hot = jnp.where(hit, 1.0, 0.0).astype(BF)
        return jnp.dot(one_hot, rows_in, preferred_element_type=F32).astype(BF).reshape(4, 64, WIDE)

    def remote(src, dst, send, recv_, to):
        return pltpu.make_async_remote_copy(
            src_ref=src, dst_ref=dst, send_sem=send, recv_sem=recv_, device_id=to, device_id_type=MESH
        )

    mine = slot(0)
    sends = []
    first = {}
    for order, d in enumerate((3, 2, 1)):
        stage[d - 1] = sort_class(cls_of(d))
        if order == 0:
            pl.semaphore_wait(barrier, len(partners))
        first[d] = remote(stage.at[d - 1], own.at[:, mine], send_sem.at[d - 1], recv_sem.at[d - 1], device(d))
        first[d].start()
    own[:, pl.ds(mine, 1)] = sort_class(cls_of(0)).reshape(4, 1, 64, WIDE)

    sib_copies, x_copies, xs_copies = {}, {}, {}
    for d in (0, 2, 1, 3):
        if d > 0:
            first[d].wait_recv()
        s = slot(d)
        sib_copies[d] = remote(own.at[:, s, :, 256:WIDE], sib.at[:, s], sib_send.at[d], sib_recv.at[d], sibling)
        sib_copies[d].start()
        x_copies[d] = [
            remote(own.at[0:2, s, :, 256:512], x_own.at[:, s, :, 0:256], x_send.at[d, 0], x_recv.at[d, 0], cross),
            remote(own.at[2:4, s, :, 512:640], x_own.at[:, s, :, 256:384], x_send.at[d, 1], x_recv.at[d, 1], cross),
        ]
        for copy in x_copies[d]:
            copy.start()
    for d in range(4):
        sib_copies[d].wait_recv()

    cls = cls_of(0)
    length = valid[slide]
    lane = iota((256, 128), 1)
    low_lane = lane < 64
    key_row = iota((256, 128), 0)
    key_step = (key_row // 64) * 2048 + lax.rem(key_row, 64) * 16

    def keys(place, group, half_, core_, a, block):
        position = key_step + (half_ * 8192 + core_ * 1024 + cls + (a % 2) * 8 + (a // 2) * 4)
        bias = jnp.where((lane == 64) & (position >= length), -1e30, 0.0).astype(BF)
        k_op[group, place : place + 256, :] = jnp.where(low_lane, block, bias)
        v_op[group, place : place + 256, :] = jnp.where(low_lane, jnp.ones_like(block), block)

    tile_of = (2, 4, 3)
    order_of = ((0, 1, 2, 3), (2, 3, 0, 1), (1, 0, 2, 3))
    for group in range(3):
        at_lane = tile_of[group] * 128
        for index, a in enumerate(order_of[group]):
            keys(index * 512, group, half, core, a, own[a, :, :, at_lane : at_lane + 128].reshape(256, 128))
            keys(index * 512 + 256, group, half, 1 - core, a, sib[a, :, :, at_lane - 256 : at_lane - 128].reshape(256, 128))
            q = own[a, :, :, (group // 2) * 128 : (group // 2) * 128 + 128].reshape(256, 128).astype(F32)
            if group == 1:
                q = pltpu.roll(q, 64, 1)
            q_op[group, a] = jnp.where(low_lane, q, jnp.where(lane == 64, 1.0, 0.0)).astype(BF)

    contract = (((1,), (1,)), ((), ()))

    def finish(group, a, acc):
        out = acc / pltpu.roll(acc, 64, 1)
        position = key_step + (half * 8192 + core * 1024 + cls + lax.rem(a, 2) * 8 + (a // 2) * 4)
        result[group, a] = jnp.where(position < length, out, 0.0)

    @pl.loop(0, 6)
    def _(tile):
        group = tile // 2
        a = lax.rem(tile, 2) + 2 * (1 - lax.rem(group, 2))
        scores = lax.dot_general(q_op[group, a], k_op[group, 0:2048, :], contract, preferred_element_type=F32)
        top = jnp.max(scores, axis=1, keepdims=True)
        expo = jnp.exp(scores - top).astype(BF)
        finish(group, a, jnp.dot(expo, v_op[group, 0:2048, :], preferred_element_type=F32))

    for d in (0, 2, 1, 3):
        s = cross_slot(d)
        for copy in x_copies[d]:
            copy.wait_recv()
        xs_copies[d] = remote(x_own.at[:, s], x_sib.at[:, s], xs_send.at[d], xs_recv.at[d], sibling)
        xs_copies[d].start()
    for d in range(4):
        xs_copies[d].wait_recv()
    for group in range(3):
        at_lane = (tile_of[group] - 2) * 128
        for index in range(2):
            a = order_of[group][index]
            keys(2048 + index * 512, group, 1 - half, core, a, x_own[a % 2, :, :, at_lane : at_lane + 128].reshape(256, 128))
            keys(2304 + index * 512, group, 1 - half, 1 - core, a, x_sib[a % 2, :, :, at_lane : at_lane + 128].reshape(256, 128))

    @pl.loop(0, 6)
    def _(tile):
        group = tile // 2
        kind = lax.rem(tile, 2)
        a = 2 * lax.rem(group, 2) + lax.rem(kind + group // 2, 2)
        extra = (1 - kind).astype(F32)
        scores = lax.dot_general(q_op[group, a], k_op[group], contract, preferred_element_type=F32)
        top = jnp.max(scores, axis=1, keepdims=True)
        expo = jnp.exp(scores - top).astype(BF)
        acc = jnp.zeros((256, 128), F32)
        for begin, end, weight in (
            (0, 512, 2.0 + extra),
            (512, 1024, 2.0),
            (1024, 2048, 1.0),
            (2048, 2560, 1.0 + extra),
            (2560, 3072, 1.0),
        ):
            acc += weight * jnp.dot(expo[:, begin:end], v_op[group, begin:end, :], preferred_element_type=F32)
        finish(group, a, acc)

    for a in range(4):
        left = jnp.where(low_lane, pltpu.roll(result[0, a], 64, 1), result[1, a])
        right = jnp.where(low_lane, pltpu.roll(result[2, a], 64, 1), 0.0)
        attn[a, :, :, 0:128] = left.astype(BF).reshape(4, 64, 128)
        attn[a, :, :, 128:256] = right.astype(BF).reshape(4, 64, 128)
    outs = []
    for d in (3, 2, 1):
        copy = remote(attn.at[:, slot(d)], back.at[cls], out_send.at[d - 1], out_recv.at[d - 1], device(d))
        copy.start()
        outs.append(copy)
    own_copy = pltpu.make_async_copy(attn.at[:, mine], back.at[cls], own_sem)
    own_copy.start()
    own_copy.wait()
    for copy in outs:
        copy.wait()
    for d in range(4):
        if d > 0:
            first[d].wait_send()
        sib_copies[d].wait_send()
        for copy in x_copies[d]:
            copy.wait_send()
        xs_copies[d].wait_send()


def attend(recv, valid):
    vmem = pl.BlockSpec(memory_space=pltpu.VMEM)
    dma = pltpu.SemaphoreType.DMA
    return pl.pallas_call(
        attend_kernel,
        out_shape=jax.ShapeDtypeStruct((4, 4, 64, 256), BF),
        in_specs=[vmem, pl.BlockSpec(memory_space=pltpu.SMEM)],
        out_specs=pl.BlockSpec(memory_space=pl.ANY),
        scratch_shapes=[
            pltpu.VMEM((4, 4, 64, WIDE), BF),
            pltpu.VMEM((4, 4, 64, 384), BF),
            pltpu.VMEM((2, 4, 64, 384), BF),
            pltpu.VMEM((2, 4, 64, 384), BF),
            pltpu.VMEM((3, 4, 64, WIDE), BF),
            pltpu.VMEM((3, 4, 256, 128), BF),
            pltpu.VMEM((3, 3072, 128), BF),
            pltpu.VMEM((3, 3072, 128), BF),
            pltpu.VMEM((3, 4, 256, 128), F32),
            pltpu.VMEM((4, 4, 64, 256), BF),
            dma((3,)),
            dma((3,)),
            dma((4,)),
            dma((4,)),
            dma((4, 2)),
            dma((4, 2)),
            dma((4,)),
            dma((4,)),
            dma((3,)),
            dma((3,)),
            dma,
        ],
        compiler_params=pltpu.CompilerParams(collective_id=1, has_side_effects=True, vmem_limit_bytes=56 * 1024 * 1024),
        name="attend",
    )(recv, valid)


def output_kernel(rows_in, weight, out, mixed):
    @pl.when(pl.program_id(0) == 0)
    def _():
        for cls in range(4):
            parts = [weight[(cls + 4 * g) * 64 : (cls + 4 * g + 1) * 64, :] for g in range(3)]
            wide = jnp.concatenate(parts + [jnp.zeros((64, D), BF)], axis=0)
            block = jnp.dot(rows_in[cls * 256 : (cls + 1) * 256, :], wide, preferred_element_type=F32)
            mixed[cls * 256 : (cls + 1) * 256, :] = block.astype(BF)

    place = iota((256, ROWS), 0) + pl.program_id(0) * 256
    step = (place >> 2) & 3
    sorted_at = (place & 3) * 256 + (((step & 1) << 1) | (step >> 1)) * 64 + (place >> 4)
    one_hot = jnp.where(sorted_at == iota((256, ROWS), 1), 1.0, 0.0).astype(BF)
    out[...] = jnp.dot(one_hot, mixed[...], preferred_element_type=F32).astype(BF)


def output(rows_in, weight):
    return pl.pallas_call(
        output_kernel,
        grid=(4,),
        out_shape=jax.ShapeDtypeStruct((ROWS, D), BF),
        in_specs=[pl.BlockSpec((ROWS, 256), lambda i: (0, 0)), pl.BlockSpec((D, D), lambda i: (0, 0))],
        out_specs=pl.BlockSpec((256, D), lambda i: (i, 0)),
        scratch_shapes=[pltpu.VMEM((ROWS, D), BF)],
        compiler_params=pltpu.CompilerParams(vmem_limit_bytes=32 * 1024 * 1024),
        name="output",
    )(rows_in, weight)


def local(tiles, destination, valid_len, in_weight, norm_gain, qkv_weight, out_weight):
    recv = project(tiles, destination.reshape(8, 128), in_weight, norm_gain.reshape(1, D), qkv_weight)
    back = attend(recv.reshape(ROWS, WIDE), valid_len)
    return output(back.reshape(ROWS, 256), out_weight).reshape(1, ROWS, D)


def solution(mesh):
    in_specs = (P(("slide", "seq"), None), P(("slide", "seq")), P(), P(), P(), P(), P())
    return jax.shard_map(local, mesh=mesh, in_specs=in_specs, out_specs=P("slide", "seq", None), check_vma=False)
```

time: 436 us -> 87.8 us (0.20); the launches traced: 430 us -> 87.3 us
  waiting for transfers between devices: 154 us -> 0 us
  local copies, waits for them, and re-layouts: 122 us -> 5.13 us
  Pallas kernels: 0 us -> 82.1 us
  other arithmetic: 66.5 us -> 0 us
  matrix products: 54.4 us -> 0 us
  starting transfers between devices: 19.1 us -> 0 us
  between operations: 14.2 us -> 0.05 us
    all_gather x6 -> x0, waiting for transfers between devices: 129 us -> none  [the longest x3 88.3 us: local(): lax.all_gather(value_rows, 'seq', axis=0, tiled=True)]
    pallas_call x0 -> x3, Pallas kernels: none -> 82.1 us  [the longest x1 44.4 us: attend(): pl.pallas_call(attend_kernel, out_shape=jax.ShapeDtypeStruct((4, 4, 64, 2...]
    dot_general x9 -> x0, matrix products: 54.4 us -> none  [the longest x3 21 us: local(): jnp.einsum('qhd,khd->hqk', query_heads, key_heads, preferred_element_type...]
    reduce_sum x9 -> x0, other arithmetic: 53.3 us -> none  [the longest x3 29.3 us: pick_rows(): jnp.sum(reshaped_input * picker[None, :, :, None], axis=1, dtype=input_ma...]
    broadcast_in_dim x27 -> x0, local copies, waits for them, and re-layouts: 44.1 us -> none  [the longest x9 37.2 us: scatter_back(): jnp.where(selected_rows[None, :, :, None], value_input[:, None], fill_value)]
    reshape x11 -> x1, local copies, waits for them, and re-layouts: 43.5 us -> 0.69 us  [local(): norm_gain.reshape(1, D)]
    all_to_all x2 -> x0, waiting for transfers between devices: 24.1 us -> none  [the longest x1 20.6 us: local(): lax.all_to_all(proj, ('slide', 'seq'), split_axis=0, concat_axis=0, tiled...]
    all_to_all x2 -> x0, starting transfers between devices: 18.6 us -> none  [the longest x1 12 us: local(): lax.all_to_all(id_parts, ('slide', 'seq'), split_axis=0, concat_axis=0, t...]
  transfers between devices with their start and end apart: 8 -> 0, of which waited for: 6 -> 0; matrix products, arithmetic and copies ran while one was open for 32% -> 0% of each run, Pallas kernels for 0% -> 0%
where the time goes in v1:
time: 87.8 us; the launch traced here: 87.3 us
  Pallas kernels  82.1 us (94%)
  local copies, waits for them, and re-layouts  5.13 us (6%)
    pallas_call x1, Pallas kernels, attend(): pl.pallas_call(attend_kernel, out_shape=jax.ShapeDtypeStruct((4, 4, 64, 2...  44.4 us
    pallas_call x1, Pallas kernels, project(): pl.pallas_call(project_kernel, out_shape=jax.ShapeDtypeStruct((DEVICES, B...  33.8 us
    unnamed x10, local copies, waits for them, and re-layouts  4.44 us
    pallas_call x1, Pallas kernels, output(): pl.pallas_call(output_kernel, grid=(4,), out_shape=jax.ShapeDtypeStruct((...  3.93 us

profile of v1, /device:TPU:1, one launch (start us, length us, event | category | flops | bytes accessed | tf_op | source)
XLA Modules:
  0.0 87.3 jit_solution(8398693998423854687)
XLA Ops:
  0.0 0.7 reshape.16.gain
  0.7 0.0 copy-start.1
  0.7 1.7 %copy-done.1 = bf16[1536,768]{1,0:T(8,128)(2,1)S(1)} copy-done((bf16[1536,768]{1,0:T(8,128)(2,1)S(1)}, bf16[1536,768]{1,0:T(8,128)(2,1)}, u32[]{:S(2)}) %copy-start.1) | copy-done | bytes 2359320
  2.4 0.0 copy-start.4
  2.4 0.7 copy-done.4
  3.0 33.8 %project_send.1 = bf16[128,8,640]{2,1,0:T(8,128)(2,1)S(1)} custom-call(bf16[1024,1536]{1,0:T(8,128)(2,1)} %tiles.1, s32[8,128]{1,0:T(8,128)S(1)} %bitcast.6, bf16[1536,768]{1,0:T(8,128)(2,1)S(1)} %copy-done.1, f32[1,768]{1,0:T(1,128)S(1)} %reshape.16.gain, bf16[768,2304]{1,0:T(8,128)(2,1)} %w_qkv.1), custom_call_target="tpu_custom_call" | custom-call | tf_op jit(solution)/shard_map/project_send/pallas_call | solution.py:138
  36.9 0.0 copy-start
  36.9 1.0 %copy-done = bf16[128,8,640]{2,1,0:T(8,128)(2,1)} copy-done((bf16[128,8,640]{2,1,0:T(8,128)(2,1)}, bf16[128,8,640]{2,1,0:T(8,128)(2,1)S(1)}, u32[]{:S(2)}) %copy-start) | copy-done | bytes 1310744
  38.0 0.0 copy-start.3
  38.0 44.4 %attend.1 = bf16[4,4,64,256]{3,2,1,0:T(8,128)(2,1)} custom-call(bf16[1024,640]{1,0:T(8,128)(2,1)} %bitcast.4, s32[8]{0:T(128)} %valid.1), custom_call_target="tpu_custom_call" | custom-call | tf_op jit(solution)/shard_map/attend/pallas_call | solution.py:340
  82.3 0.0 copy-done.3
  82.3 0.0 copy-start.2
  82.3 1.0 %copy-done.2 = bf16[4,4,64,256]{3,2,1,0:T(8,128)(2,1)S(1)} copy-done((bf16[4,4,64,256]{3,2,1,0:T(8,128)(2,1)S(1)}, bf16[4,4,64,256]{3,2,1,0:T(8,128)(2,1)}, u32[]{:S(2)}) %copy-start.2) | copy-done | bytes 524312
  83.4 3.9 %output.1 = bf16[1024,768]{1,0:T(8,128)(2,1)} custom-call(bf16[1024,256]{1,0:T(8,128)(2,1)S(1)} %bitcast.5, bf16[768,768]{1,0:T(8,128)(2,1)S(1)} %copy-done.3), custom_call_target="tpu_custom_call" | custom-call | tf_op jit(solution)/shard_map/output/pallas_call | solution.py:390
Async XLA Ops:
  0.7 1.7 %copy-start.1 = (bf16[1536,768]{1,0:T(8,128)(2,1)S(1)}, bf16[1536,768]{1,0:T(8,128)(2,1)}, u32[]{:S(2)}) copy-start(bf16[1536,768]{1,0:T(8,128)(2,1)} %w_in.1) | copy-start | bytes 7077892
  2.4 0.7 copy-start.4
  36.9 1.1 %copy-start = (bf16[128,8,640]{2,1,0:T(8,128)(2,1)}, bf16[128,8,640]{2,1,0:T(8,128)(2,1)S(1)}, u32[]{:S(2)}) copy-start(bf16[128,8,640]{2,1,0:T(8,128)(2,1)S(1)} %project_send.1) | copy-start | bytes 3932164
  38.0 44.4 %copy-start.3 = (bf16[768,768]{1,0:T(8,128)(2,1)S(1)}, bf16[768,768]{1,0:T(8,128)(2,1)}, u32[]{:S(2)}) copy-start(bf16[768,768]{1,0:T(8,128)(2,1)} %weight.1) | copy-start | bytes 3538948
  82.3 1.0 %copy-start.2 = (bf16[4,4,64,256]{3,2,1,0:T(8,128)(2,1)S(1)}, bf16[4,4,64,256]{3,2,1,0:T(8,128)(2,1)}, u32[]{:S(2)}) copy-start(bf16[4,4,64,256]{3,2,1,0:T(8,128)(2,1)} %attend.1) | copy-start | bytes 1572868

commit v2 on v1

v2 whole, which is shorter than its diff:
```python
import functools

import jax
import jax.numpy as jnp
from jax import lax
from jax.experimental import pallas as pl
from jax.experimental.pallas import tpu as pltpu
from jax.sharding import PartitionSpec as P

MESH = pl.DeviceIdType.MESH
SLIDES = 8
SEQ = 16
DEVICES = 128
ROWS = 1024
BLOCK = 8
E = 1536
D = 768
WIDE = 640
PLACES = 4
VMEM_LIMIT = 63 * 1024 * 1024
CHUNK = 256
BF = jnp.bfloat16
F32 = jnp.float32
I32 = jnp.int32


def iota(shape, dim):
    return lax.broadcasted_iota(I32, shape, dim)


def pick_columns(qkv, place):
    rows = qkv.shape[0]
    lane = iota((rows, 128), 1)
    cls = place & 3
    high = cls >= 2
    odd = (cls & 1) == 1
    low_lane = lane < 64

    def head(kind, group):
        at = kind * D + group * 256
        return jnp.where(high, qkv[:, at + 128 : at + 256], qkv[:, at : at + 128])

    def pair(left, right):
        moved = pltpu.roll(jnp.where(odd, left, right), 64, 1)
        return jnp.where(low_lane == odd, moved, jnp.where(odd, right, left))

    step = (place >> 2) & 3
    sorted_at = cls * 256 + (((step & 1) << 1) | (step >> 1)) * 64 + (place >> 4)
    ids = jnp.where(lane == 64, sorted_at >> 7, jnp.where(lane == 65, sorted_at & 127, 0)).astype(F32)
    q2 = head(0, 2) * 0.125
    q2 = jnp.where(odd, pltpu.roll(q2, 64, 1), q2)
    return (
        pair(head(0, 0) * 0.125, head(0, 1) * 0.125),
        jnp.where(low_lane, q2, ids),
        pair(head(1, 0), head(2, 0)),
        pair(head(1, 2), head(2, 2)),
        pair(head(1, 1), head(2, 1)),
    )


def project_kernel(tiles, dest, w_in, gain, w_qkv, recv, tiles_v, w_in_v, w_qkv_v, dest_v, gain_v, send, load_sem, send_sem, recv_sem, own_sem):
    slide = lax.axis_index("slide")
    seq = lax.axis_index("seq")
    me = slide * SEQ + seq
    across = seq // PLACES
    place_me = lax.rem(seq, PLACES)

    def place_at(step):
        return lax.rem(place_me + step, PLACES)

    loads = [
        pltpu.make_async_copy(w_in, w_in_v, load_sem.at[0]),
        pltpu.make_async_copy(w_qkv, w_qkv_v, load_sem.at[1]),
        pltpu.make_async_copy(dest, dest_v, load_sem.at[2]),
        pltpu.make_async_copy(gain, gain_v, load_sem.at[3]),
    ]
    for step in range(PLACES):
        loads.append(pltpu.make_async_copy(tiles.at[:, place_at(step)], tiles_v.at[step], load_sem.at[4 + step]))
    for index in (0, 4, 2, 3, 1, 5, 6, 7):
        loads[index].start()

    barrier = pltpu.get_barrier_semaphore()

    @pl.loop(1, DEVICES)
    def _(i):
        other = lax.rem(me + i, DEVICES)
        pl.semaphore_signal(barrier, inc=1, device_id=(other // SEQ, lax.rem(other, SEQ)), device_id_type=MESH)

    for step in range(PLACES):
        place = place_at(step)
        if step == 0:
            loads[0].wait()
        loads[4 + step].wait()
        x = tiles_v[step].reshape(CHUNK, E)
        proj = jnp.dot(x, w_in_v[...], preferred_element_type=F32).astype(BF).astype(F32)
        mean = jnp.mean(proj, axis=-1, keepdims=True)
        centred = proj - mean
        var = jnp.mean(centred * centred, axis=-1, keepdims=True)
        if step == 0:
            loads[3].wait()
        gains = jnp.concatenate([gain_v[i : i + 1, :] for i in range(D // 128)], axis=1)
        normed = (centred * lax.rsqrt(var + 1e-05) * gains).astype(BF)
        if step == 0:
            loads[1].wait()
        qkv = jnp.dot(normed, w_qkv_v[...], preferred_element_type=F32)
        if step == 0:
            loads[2].wait()
        lines = (dest_v[...] & (ROWS - 1)).astype(F32)
        lines = jnp.broadcast_to(lines.reshape(8, 1, 128), (8, 32, 128)).reshape(CHUNK, 128)
        r = iota((CHUNK, 128), 0)
        wanted = ((r >> 3) & 3) * 32 + place * 8 + (r & 7)
        position = jnp.sum(jnp.where(iota((CHUNK, 128), 1) == wanted, lines, 0.0), axis=1, keepdims=True).astype(I32)
        for index, block in enumerate(pick_columns(qkv, position)):
            send[:, place, :, index * 128 : (index + 1) * 128] = block.reshape(CHUNK // BLOCK, BLOCK, 128).astype(BF)
        if step == 0:
            pl.semaphore_wait(barrier, DEVICES - 1)

        @pl.loop(0, CHUNK // BLOCK)
        def _(i):
            to_slide = lax.rem(slide + i, SLIDES)
            to_across = lax.rem(across + i // SLIDES, 4)

            @pl.when((to_slide != slide) | (to_across != across) | (place != place_me))
            def _():
                pltpu.make_async_remote_copy(
                    src_ref=send.at[to_slide * 4 + to_across, place],
                    dst_ref=recv.at[me],
                    send_sem=send_sem,
                    recv_sem=recv_sem,
                    device_id=(to_slide, to_across * PLACES + place),
                    device_id_type=MESH,
                ).start()

    own = pltpu.make_async_copy(send.at[slide * 4 + across, place_me], recv.at[me], own_sem)
    own.start()
    own.wait()
    rest = pl.ds(0, DEVICES - 1)
    pltpu.make_async_copy(recv.at[rest], recv.at[rest], send_sem).wait()
    pltpu.make_async_copy(recv.at[rest], recv.at[rest], recv_sem).wait()


def project(tiles, dest, w_in, gain, w_qkv):
    hbm = pl.BlockSpec(memory_space=pltpu.HBM)
    return pl.pallas_call(
        project_kernel,
        out_shape=jax.ShapeDtypeStruct((DEVICES, BLOCK, WIDE), BF),
        in_specs=[hbm] * 5,
        out_specs=hbm,
        scratch_shapes=[
            pltpu.VMEM((PLACES, CHUNK // BLOCK, BLOCK, E), BF),
            pltpu.VMEM((E, D), BF),
            pltpu.VMEM((D, 3 * D), BF),
            pltpu.VMEM((8, 128), I32),
            pltpu.VMEM((D // 128, 128), F32),
            pltpu.VMEM((CHUNK // BLOCK, PLACES, BLOCK, WIDE), BF),
            pltpu.SemaphoreType.DMA((4 + PLACES,)),
            pltpu.SemaphoreType.DMA,
            pltpu.SemaphoreType.DMA,
            pltpu.SemaphoreType.DMA,
        ],
        compiler_params=pltpu.CompilerParams(collective_id=0, has_side_effects=True, vmem_limit_bytes=VMEM_LIMIT),
        name="project_send",
    )(tiles, dest, w_in, gain, w_qkv)


ARRIVAL = (0, 2, 1, 3)
TILE_OF = (2, 4, 3)
PAIR_OF = ((0, 1), (2, 3), (1, 0))
LN2 = (0.69140625, 0.0017409306)
LN3 = (1.1015625, -0.0029502113)


def key_table(rows, group, key_first, inner):
    lane = iota((rows, 128), 1)
    key = iota((rows, 128), 0) // 64 + key_first
    third, second = PAIR_OF[group]
    query = jnp.where(lane < 69, lane - 65, lane - 69)
    used = (lane >= 65) & (lane < 73)
    twice = used & ((query == third) | (query == second)) & ((key == third) | (key == second))
    thrice = used & (query == third) & (key == third)
    first = lane < 69
    ln2 = jnp.where(first, LN2[0], LN2[1])
    ln3 = jnp.where(first, LN3[0], LN3[1])
    if inner:
        return jnp.where(thrice, ln3, jnp.where(twice, ln2, 0.0))
    return jnp.where(thrice, ln2, 0.0)


def attend_kernel(
    recv, valid, back, own, sib, x_own, x_sib, stage, q_op, k_op, v_op, xk_op, xv_op, tops, sums, attn, q_tab, k_tab, x_tab,
    send_sem, recv_sem, sib_send, sib_recv, x_send, x_recv, xs_send, xs_recv, out_send, out_recv, own_sem,
):
    slide = lax.axis_index("slide")
    seq = lax.axis_index("seq")
    half = seq // 8
    row = lax.rem(seq // 4, 2)
    col = lax.rem(seq // 2, 2)
    core = lax.rem(seq, 2)

    def slot(d):
        return 2 * lax.rem(row + d // 2, 2) + lax.rem(col + d % 2, 2)

    def cross_slot(d):
        return 2 * lax.rem(1 - row + d // 2, 2) + lax.rem(col + d % 2, 2)

    def cls_of(d):
        return 2 * lax.rem(row + d // 2 + half, 2) + lax.rem(col + d % 2, 2)

    def device(d):
        return (slide, half * 8 + slot(d) * 2 + core)

    sibling = (slide, seq + 1 - 2 * core)
    cross = (slide, (1 - half) * 8 + cross_slot(0) * 2 + core)
    partners = [device(1), device(2), device(3), sibling, cross]

    barrier = pltpu.get_barrier_semaphore()
    for other in partners:
        pl.semaphore_signal(barrier, inc=1, device_id=other, device_id_type=MESH)

    rows_in = recv[...]
    lane8 = iota((8, 128), 1)
    weigh = jnp.where(lane8 == 64, 128.0, jnp.where(lane8 == 65, 1.0, 0.0)).astype(BF)
    at = lax.dot_general(weigh, rows_in[:, 128:256], (((1,), (1,)), ((), ())), preferred_element_type=F32)
    at = at[0:1].astype(I32)

    def sort_class(cls):
        hit = (at - cls * 256) == iota((256, ROWS), 0)
        one_hot = jnp.where(hit, 1.0, 0.0).astype(BF)
        return jnp.dot(one_hot, rows_in, preferred_element_type=F32).astype(BF).reshape(4, 64, WIDE)

    def remote(src, dst, send, recv_, to):
        return pltpu.make_async_remote_copy(
            src_ref=src, dst_ref=dst, send_sem=send, recv_sem=recv_, device_id=to, device_id_type=MESH
        )

    first = {}
    for order, d in enumerate(ARRIVAL[1:]):
        stage[d - 1] = sort_class(cls_of(d))
        if order == 0:
            pl.semaphore_wait(barrier, len(partners))
        first[d] = remote(stage.at[d - 1], own.at[d], send_sem.at[d - 1], recv_sem.at[d - 1], device(d))
        first[d].start()
    own[0] = sort_class(cls_of(0))

    sib_copies, x_copies, xs_copies = {}, {}, {}

    def arrive(d):
        if d > 0:
            first[d].wait_recv()
        sib_copies[d] = remote(own.at[d, :, :, 256:WIDE], sib.at[d], sib_send.at[d], sib_recv.at[d], sibling)
        sib_copies[d].start()
        x_copies[d] = [
            remote(own.at[d, 0:2, :, 256:512], x_own.at[d, :, :, 0:256], x_send.at[d, 0], x_recv.at[d, 0], cross),
            remote(own.at[d, 2:4, :, 512:640], x_own.at[d, :, :, 256:384], x_send.at[d, 1], x_recv.at[d, 1], cross),
        ]
        for copy in x_copies[d]:
            copy.start()

    def arrive_cross(d):
        for copy in x_copies[d]:
            copy.wait_recv()
        xs_copies[d] = remote(x_own.at[d], x_sib.at[d], xs_send.at[d], xs_recv.at[d], sibling)
        xs_copies[d].start()

    cls = cls_of(0)
    length = valid[slide]
    lane = iota((256, 128), 1)
    low_lane = lane < 64
    line = iota((256, 128), 0)
    residue = line // 64
    steps = lax.rem(line, 64) * 16 + lax.rem(residue, 2) * 8 + (residue // 2) * 4

    def start_of(half_, slot_, core_):
        return half_ * 8192 + slot_ * 2048 + core_ * 1024 + cls

    q_tab[...] = jnp.where((lane == 64) | (lane == 65 + residue) | (lane == 69 + residue), 1.0, 0.0).astype(BF)
    for group in range(3):
        k_tab[group] = key_table(256, group, 0, True).astype(BF)
        x_tab[group] = key_table(128, group, 2 * (group % 2), False).astype(BF)

    def prepare(e):
        d = ARRIVAL[e]
        sib_copies[d].wait_recv()
        for source, core_ in ((own, core), (sib, 1 - core)):
            masked = (lane == 64) & (steps + start_of(half, slot(d), core_) >= length)
            at_row = e * 512 + (0 if source is own else 256)
            for group in range(3):
                at_lane = TILE_OF[group] * 128 - (0 if source is own else 256)
                block = source[d, :, :, at_lane : at_lane + 128].reshape(256, 128)
                bias = jnp.where(masked, jnp.full_like(block, -1e30), k_tab[group])
                k_op[group, at_row : at_row + 256, :] = jnp.where(low_lane, block, bias)
                v_op[group, at_row : at_row + 256, :] = jnp.where(low_lane, jnp.ones_like(block), block)
        for group in range(3):
            at_lane = (group // 2) * 128
            q = own[d, :, :, at_lane : at_lane + 128].reshape(256, 128)
            if group == 1:
                q = pltpu.roll(q.astype(F32), 64, 1).astype(BF)
            q_op[group, e] = jnp.where(low_lane, q, q_tab[...])

    def prepare_cross(e):
        d = ARRIVAL[e]
        xs_copies[d].wait_recv()
        for source, core_ in ((x_own, core), (x_sib, 1 - core)):
            at_row = e * 256 + (0 if source is x_own else 128)
            for group in range(3):
                at_lane = TILE_OF[group] * 128 - 256
                block = source[d, :, :, at_lane : at_lane + 128].reshape(128, 128)
                position = steps[0:128] + start_of(1 - half, cross_slot(d), core_) + 4 * (group % 2)
                masked = (lane[0:128] == 64) & (position >= length)
                bias = jnp.where(masked, jnp.full_like(block, -1e30), x_tab[group])
                xk_op[group, at_row : at_row + 128, :] = jnp.where(low_lane[0:128], block, bias)
                xv_op[group, at_row : at_row + 128, :] = jnp.where(low_lane[0:128], jnp.ones_like(block), block)

    contract = (((1,), (1,)), ((), ()))

    def wide(column, count):
        return jnp.concatenate([column] * count, axis=1)

    def mix(q, keys, values, state):
        scores = lax.dot_general(q, keys, contract, preferred_element_type=F32)
        top = jnp.broadcast_to(jnp.max(scores, axis=1, keepdims=True), (q.shape[0], 128))
        if state is not None:
            top = jnp.maximum(state[0], top)
        expo = jnp.exp(scores - wide(top, scores.shape[1] // 128)).astype(BF)
        acc = jnp.dot(expo, values, preferred_element_type=F32)
        if state is not None:
            acc += state[1] * jnp.exp(state[0] - top)
        return top, acc

    def parts(group, todo):
        states = [None if fresh else (tops[group, e], sums[group, e]) for e, _, _, fresh in todo]
        found = [
            mix(q_op[group, e], k_op[group, begin:end, :], v_op[group, begin:end, :], state)
            for (e, begin, end, _), state in zip(todo, states)
        ]
        for (e, _, _, _), (top, acc) in zip(todo, found):
            tops[group, e] = top
            sums[group, e] = acc

    def cross_parts(groups, begin, end):
        todo = []
        for group in groups:
            rows = pl.ds(pl.multiple_of(128 * lax.rem(group, 2), 128), 128)
            for both in ((0, 1), (2, 3)):
                todo.append((group, rows, both))

        def load(ref, group, rows, both):
            return jnp.concatenate([ref[group, e, rows, :] for e in both], axis=0)

        states = [(load(tops, *what), load(sums, *what)) for what in todo]
        queries = [load(q_op, *what) for what in todo]
        found = [
            mix(q, xk_op[what[0], begin:end, :], xv_op[what[0], begin:end, :], state)
            for what, q, state in zip(todo, queries, states)
        ]
        for (group, rows, both), (top, acc) in zip(todo, found):
            for index, e in enumerate(both):
                tops[group, e, rows, :] = top[index * 128 : index * 128 + 128]
                sums[group, e, rows, :] = acc[index * 128 : index * 128 + 128]

    arrive(0)
    prepare(0)
    for group in range(3):
        parts(group, [(0, 0, 512, True)])
    arrive(2)
    arrive(1)
    prepare(1)
    prepare(2)

    @pl.loop(0, 3)
    def _(group):
        parts(group, [(0, 512, 1536, False), (1, 0, 1536, True), (2, 0, 1536, True)])

    arrive(3)
    for d in (0, 2, 1):
        arrive_cross(d)
    prepare(3)

    @pl.loop(0, 3)
    def _(group):
        parts(group, [(3, 0, 2048, True)] + [(e, 1536, 2048, False) for e in range(3)])

    def finish(group, e, begin):
        acc = sums[group, e, begin : begin + 128, :]
        position = steps[begin : begin + 128] + start_of(half, slot(ARRIVAL[e]), core)
        return jnp.where(position < length, acc / pltpu.roll(acc, 64, 1), 0.0)

    outs = []

    def give(turn):
        wide, narrow = (128, 0) if turn == 0 else (0, 128)
        for e in (3, 1, 2, 0):
            d = ARRIVAL[e]
            low, high = finish(0, e, wide), finish(2, e, wide)
            middle = finish(1, e, narrow)
            joined = jnp.where(low_lane[0:128], pltpu.roll(low, 64, 1), high)
            packed = jnp.where(low_lane[0:64], pltpu.roll(middle[0:64], 64, 1), middle[64:128])
            attn[d, 3 * turn : 3 * turn + 2] = joined.astype(BF).reshape(2, 64, 128)
            attn[d, 3 * turn + 2] = packed.astype(BF)
            src, dst = attn.at[d, pl.ds(3 * turn, 3)], back.at[cls, pl.ds(3 * turn, 3)]
            if d > 0:
                copy = remote(src, dst, out_send.at[turn, d - 1], out_recv.at[turn, d - 1], device(d))
            else:
                copy = pltpu.make_async_copy(src, dst, own_sem.at[turn])
            copy.start()
            outs.append(copy)

    give(0)
    arrive_cross(3)
    for e in range(3):
        prepare_cross(e)

    @pl.loop(0, 3)
    def _(group):
        cross_parts([group], 0, 768)

    prepare_cross(3)
    cross_parts(range(3), 768, 1024)
    give(1)
    for copy in outs:
        copy.wait()
    for d in range(4):
        if d > 0:
            first[d].wait_send()
        sib_copies[d].wait_send()
        for copy in x_copies[d]:
            copy.wait_send()
        xs_copies[d].wait_send()


def attend(recv, valid):
    vmem = pl.BlockSpec(memory_space=pltpu.VMEM)
    dma = pltpu.SemaphoreType.DMA
    return pl.pallas_call(
        attend_kernel,
        out_shape=jax.ShapeDtypeStruct((4, 6, 64, 128), BF),
        in_specs=[vmem, pl.BlockSpec(memory_space=pltpu.SMEM)],
        out_specs=pl.BlockSpec(memory_space=pltpu.HBM),
        scratch_shapes=[
            pltpu.VMEM((4, 4, 64, WIDE), BF),
            pltpu.VMEM((4, 4, 64, 384), BF),
            pltpu.VMEM((4, 2, 64, 384), BF),
            pltpu.VMEM((4, 2, 64, 384), BF),
            pltpu.VMEM((3, 4, 64, WIDE), BF),
            pltpu.VMEM((3, 4, 256, 128), BF),
            pltpu.VMEM((3, 2048, 128), BF),
            pltpu.VMEM((3, 2048, 128), BF),
            pltpu.VMEM((3, 1024, 128), BF),
            pltpu.VMEM((3, 1024, 128), BF),
            pltpu.VMEM((3, 4, 256, 128), F32),
            pltpu.VMEM((3, 4, 256, 128), F32),
            pltpu.VMEM((4, 6, 64, 128), BF),
            pltpu.VMEM((256, 128), BF),
            pltpu.VMEM((3, 256, 128), BF),
            pltpu.VMEM((3, 128, 128), BF),
            dma((3,)),
            dma((3,)),
            dma((4,)),
            dma((4,)),
            dma((4, 2)),
            dma((4, 2)),
            dma((4,)),
            dma((4,)),
            dma((2, 3)),
            dma((2, 3)),
            dma((2,)),
        ],
        compiler_params=pltpu.CompilerParams(collective_id=1, has_side_effects=True, vmem_limit_bytes=VMEM_LIMIT),
        name="attend",
    )(recv, valid)


def output_kernel(rows_in, weight, out, mixed):
    @pl.when(pl.program_id(0) == 0)
    def _():
        for cls in range(4):
            w0, w1, w2 = [weight[(cls + 4 * g) * 64 : (cls + 4 * g + 1) * 64, :] for g in range(3)]
            zero = jnp.zeros((64, D), BF)
            w02 = jnp.concatenate([w0, w2], axis=0)
            ends = (jnp.concatenate([w1, zero], axis=0), jnp.concatenate([zero, w1], axis=0))
            rows = jnp.concatenate([rows_in[cls, i] for i in (3, 4, 0, 1)], axis=0)
            block = jnp.dot(rows, w02, preferred_element_type=F32)
            for a in range(4):
                middle = rows_in[cls, 2 if a < 2 else 5]
                total = block[a * 64 : a * 64 + 64] + jnp.dot(middle, ends[a % 2], preferred_element_type=F32)
                mixed[cls * 256 + a * 64 : cls * 256 + a * 64 + 64, :] = total.astype(BF)

    place = iota((256, ROWS), 0) + pl.program_id(0) * 256
    step = (place >> 2) & 3
    sorted_at = (place & 3) * 256 + (((step & 1) << 1) | (step >> 1)) * 64 + (place >> 4)
    one_hot = jnp.where(sorted_at == iota((256, ROWS), 1), 1.0, 0.0).astype(BF)
    out[...] = jnp.dot(one_hot, mixed[...], preferred_element_type=F32).astype(BF)


def output(rows_in, weight):
    return pl.pallas_call(
        output_kernel,
        grid=(4,),
        out_shape=jax.ShapeDtypeStruct((ROWS, D), BF),
        in_specs=[pl.BlockSpec((4, 6, 64, 128), lambda i: (0, 0, 0, 0)), pl.BlockSpec((D, D), lambda i: (0, 0))],
        out_specs=pl.BlockSpec((256, D), lambda i: (i, 0)),
        scratch_shapes=[pltpu.VMEM((ROWS, D), BF)],
        compiler_params=pltpu.CompilerParams(vmem_limit_bytes=32 * 1024 * 1024),
        name="output",
    )(rows_in, weight)


def local(tiles, destination, valid_len, in_weight, norm_gain, qkv_weight, out_weight):
    recv = project(tiles.reshape(CHUNK // BLOCK, PLACES, BLOCK, E), destination.reshape(8, 128), in_weight, norm_gain.reshape(D // 128, 128), qkv_weight)
    back = attend(recv.reshape(ROWS, WIDE), valid_len)
    return output(back, out_weight).reshape(1, ROWS, D)


def solution(mesh):
    in_specs = (P(("slide", "seq"), None), P(("slide", "seq")), P(), P(), P(), P(), P())
    return jax.shard_map(local, mesh=mesh, in_specs=in_specs, out_specs=P("slide", "seq", None), check_vma=False)
```

time: 87.8 us -> 78.2 us (0.89)
  Pallas kernels: 82.1 us -> 75.1 us
  local copies, waits for them, and re-layouts: 5.13 us -> 2.26 us
    pallas_call x1, Pallas kernels: 33.8 us -> 30 us  [project(): pl.pallas_call(project_kernel, out_shape=jax.ShapeDtypeStruct((DEVICES, B...]
    pallas_call x1, Pallas kernels: 44.4 us -> 40.8 us  [attend(): pl.pallas_call(attend_kernel, out_shape=jax.ShapeDtypeStruct((4, 6, 64, 1...]
    unnamed x10 -> x4, local copies, waits for them, and re-layouts: 4.44 us -> 2.26 us
where the time goes in v2:
time: 78.2 us; the launch traced here: 77.4 us
  Pallas kernels  75.1 us (96%)
  local copies, waits for them, and re-layouts  2.26 us (3%)
    pallas_call x1, Pallas kernels, attend(): pl.pallas_call(attend_kernel, out_shape=jax.ShapeDtypeStruct((4, 6, 64, 1...  40.8 us
    pallas_call x1, Pallas kernels, project(): pl.pallas_call(project_kernel, out_shape=jax.ShapeDtypeStruct((DEVICES, B...  30 us
    pallas_call x1, Pallas kernels, output(): pl.pallas_call(output_kernel, grid=(4,), out_shape=jax.ShapeDtypeStruct((...  4.33 us
    unnamed x4, local copies, waits for them, and re-layouts  2.26 us

profile of v2, /device:TPU:1, one launch (start us, length us, event | category | flops | bytes accessed | tf_op | source)
XLA Modules:
  0.0 77.4 jit_solution(709926789652878559)
XLA Ops:
  0.0 30.0 %project_send.1 = bf16[128,8,640]{2,1,0:T(8,128)(2,1)} custom-call(bf16[32,4,8,1536]{3,2,1,0:T(8,128)(2,1)} %bitcast.6, s32[8,128]{1,0:T(8,128)} %bitcast.7, bf16[1536,768]{1,0:T(8,128)(2,1)} %w_in.1, f32[6,128]{1,0:T(8,128)} %bitcast.8, bf16[768,2304]{1,0:T(8,128)(2,1)} %w_qkv.1), custom_call_target="tpu_custom_call" | custom-call | tf_op jit(solution)/shard_map/project_send/pallas_call | solution.py:144
  30.0 40.8 %attend.1.rows_in = bf16[4,6,64,128]{3,2,1,0:T(8,128)(2,1)} custom-call(bf16[1024,640]{1,0:T(8,128)(2,1)} %bitcast.5, s32[8]{0:T(128)} %valid.1), custom_call_target="tpu_custom_call" | custom-call | tf_op jit(solution)/shard_map/attend/pallas_call | solution.py:434
  70.8 0.0 copy-start
  70.8 1.0 %copy-done = bf16[4,6,64,128]{3,2,1,0:T(8,128)(2,1)S(1)} copy-done((bf16[4,6,64,128]{3,2,1,0:T(8,128)(2,1)S(1)}, bf16[4,6,64,128]{3,2,1,0:T(8,128)(2,1)}, u32[]{:S(2)}) %copy-start) | copy-done | bytes 393240
  71.8 0.0 copy-start.1
  71.8 1.3 %copy-done.1 = bf16[768,768]{1,0:T(8,128)(2,1)S(1)} copy-done((bf16[768,768]{1,0:T(8,128)(2,1)S(1)}, bf16[768,768]{1,0:T(8,128)(2,1)}, u32[]{:S(2)}) %copy-start.1) | copy-done | bytes 1179672
  73.0 4.3 %output.1 = bf16[1024,768]{1,0:T(8,128)(2,1)} custom-call(bf16[4,6,64,128]{3,2,1,0:T(8,128)(2,1)S(1)} %copy-done, bf16[768,768]{1,0:T(8,128)(2,1)S(1)} %copy-done.1), custom_call_target="tpu_custom_call" | custom-call | tf_op jit(solution)/shard_map/output/pallas_call | solution.py:496
Async XLA Ops:
  70.8 1.0 %copy-start = (bf16[4,6,64,128]{3,2,1,0:T(8,128)(2,1)S(1)}, bf16[4,6,64,128]{3,2,1,0:T(8,128)(2,1)}, u32[]{:S(2)}) copy-start(bf16[4,6,64,128]{3,2,1,0:T(8,128)(2,1)} %attend.1.rows_in) | copy-start | bytes 1179652
  71.8 1.3 %copy-start.1 = (bf16[768,768]{1,0:T(8,128)(2,1)S(1)}, bf16[768,768]{1,0:T(8,128)(2,1)}, u32[]{:S(2)}) copy-start(bf16[768,768]{1,0:T(8,128)(2,1)} %weight.1) | copy-start | bytes 3538948

commit v3 on v2

--- a/solution.py
+++ b/solution.py
@@ -164,19 +164,19 @@
 
 
 ARRIVAL = (0, 2, 1, 3)
-TILE_OF = (2, 4, 3)
 PAIR_OF = ((0, 1), (2, 3), (1, 0))
 LN2 = (0.69140625, 0.0017409306)
 LN3 = (1.1015625, -0.0029502113)
-
-
-def key_table(rows, group, key_first, inner):
-    lane = iota((rows, 128), 1)
-    key = iota((rows, 128), 0) // 64 + key_first
+PAIRS = (0, 4, 2)
+
+
+def key_table(group, inner):
+    lane = iota((128, 128), 1)
+    key = iota((128, 128), 0) // 64 + 2 * (group % 2)
     third, second = PAIR_OF[group]
     query = jnp.where(lane < 69, lane - 65, lane - 69)
     used = (lane >= 65) & (lane < 73)
-    twice = used & ((query == third) | (query == second)) & ((key == third) | (key == second))
+    twice = used & ((query == third) | (query == second))
     thrice = used & (query == third) & (key == third)
     first = lane < 69
     ln2 = jnp.where(first, LN2[0], LN2[1])
@@ -222,179 +222,199 @@
     weigh = jnp.where(lane8 == 64, 128.0, jnp.where(lane8 == 65, 1.0, 0.0)).astype(BF)
     at = lax.dot_general(weigh, rows_in[:, 128:256], (((1,), (1,)), ((), ())), preferred_element_type=F32)
     at = at[0:1].astype(I32)
-
-    def sort_class(cls):
+    low64 = iota((64, 128), 1) < 64
+
+    def sort_class(cls, ref):
         hit = (at - cls * 256) == iota((256, ROWS), 0)
         one_hot = jnp.where(hit, 1.0, 0.0).astype(BF)
-        return jnp.dot(one_hot, rows_in, preferred_element_type=F32).astype(BF).reshape(4, 64, WIDE)
+        found = jnp.dot(one_hot, rows_in, preferred_element_type=F32)
+
+        def tile(a, t):
+            return found[a * 64 : a * 64 + 64, t * 128 : t * 128 + 128]
+
+        for index, (t, a) in enumerate(((2, 0), (3, 0), (4, 2))):
+            for i in range(2):
+                ref[2 * index + i] = tile(a + i, t).astype(BF)
+                ref[12 + 2 * index + i] = tile((a + 2) % 4 + i, t).astype(BF)
+        for a in range(4):
+            ref[6 + a] = tile(a, 0).astype(BF)
+        for i in range(2):
+            ref[10 + i] = jnp.where(low64, tile(2 * i, 1), pltpu.roll(tile(2 * i + 1, 1), 64, 1)).astype(BF)
 
     def remote(src, dst, send, recv_, to):
         return pltpu.make_async_remote_copy(
             src_ref=src, dst_ref=dst, send_sem=send, recv_sem=recv_, device_id=to, device_id_type=MESH
         )
 
-    first = {}
+    third = {}
+
+    def send(d, turn):
+        part = pl.ds(6 * turn, 6)
+        copy = remote(
+            stage.at[d - 1, part], own.at[d, part], send_sem.at[d - 1, turn], recv_sem.at[d - 1, turn], device(d)
+        )
+        copy.start()
+        third[d, turn] = copy
+
     for order, d in enumerate(ARRIVAL[1:]):
-        stage[d - 1] = sort_class(cls_of(d))
+        sort_class(cls_of(d), stage.at[d - 1])
         if order == 0:
             pl.semaphore_wait(barrier, len(partners))
-        first[d] = remote(stage.at[d - 1], own.at[d], send_sem.at[d - 1], recv_sem.at[d - 1], device(d))
-        first[d].start()
-    own[0] = sort_class(cls_of(0))
+        send(d, 0)
+    sort_class(cls_of(0), own.at[0])
 
     sib_copies, x_copies, xs_copies = {}, {}, {}
 
-    def arrive(d):
+    def share(d, turn):
         if d > 0:
-            first[d].wait_recv()
-        sib_copies[d] = remote(own.at[d, :, :, 256:WIDE], sib.at[d], sib_send.at[d], sib_recv.at[d], sibling)
-        sib_copies[d].start()
-        x_copies[d] = [
-            remote(own.at[d, 0:2, :, 256:512], x_own.at[d, :, :, 0:256], x_send.at[d, 0], x_recv.at[d, 0], cross),
-            remote(own.at[d, 2:4, :, 512:640], x_own.at[d, :, :, 256:384], x_send.at[d, 1], x_recv.at[d, 1], cross),
-        ]
-        for copy in x_copies[d]:
-            copy.start()
-
-    def arrive_cross(d):
-        for copy in x_copies[d]:
-            copy.wait_recv()
+            third[d, turn].wait_recv()
+        to = 0 if turn == 0 else 6
+        copy = remote(
+            own.at[d, pl.ds(6 * turn, 6)], sib.at[d, pl.ds(to, 6)], sib_send.at[d, to // 6], sib_recv.at[d, to // 6], sibling
+        )
+        copy.start()
+        sib_copies[d, turn] = copy
+        if turn == 0:
+            x_copies[d] = remote(own.at[d, pl.ds(0, 6)], x_own.at[d], x_send.at[d], x_recv.at[d], cross)
+            x_copies[d].start()
+
+    def share_cross(d):
+        x_copies[d].wait_recv()
         xs_copies[d] = remote(x_own.at[d], x_sib.at[d], xs_send.at[d], xs_recv.at[d], sibling)
         xs_copies[d].start()
 
     cls = cls_of(0)
     length = valid[slide]
-    lane = iota((256, 128), 1)
+    lane = iota((128, 128), 1)
     low_lane = lane < 64
-    line = iota((256, 128), 0)
-    residue = line // 64
-    steps = lax.rem(line, 64) * 16 + lax.rem(residue, 2) * 8 + (residue // 2) * 4
+    line = iota((128, 128), 0)
+    steps = lax.rem(line, 64) * 16 + (line // 64) * 8
 
     def start_of(half_, slot_, core_):
         return half_ * 8192 + slot_ * 2048 + core_ * 1024 + cls
 
-    q_tab[...] = jnp.where((lane == 64) | (lane == 65 + residue) | (lane == 69 + residue), 1.0, 0.0).astype(BF)
+    for pair in range(2):
+        residue = line // 64 + 2 * pair
+        ones = jnp.where((lane == 64) | (lane == 65 + residue) | (lane == 69 + residue), 1.0, 0.0)
+        q_tab[pair] = ones.astype(BF)
     for group in range(3):
-        k_tab[group] = key_table(256, group, 0, True).astype(BF)
-        x_tab[group] = key_table(128, group, 2 * (group % 2), False).astype(BF)
-
-    def prepare(e):
+        k_tab[group] = key_table(group, True).astype(BF)
+        x_tab[group] = key_table(group, False).astype(BF)
+
+    def keys(k_ref, v_ref, group, at_row, block, position, table):
+        block = block.reshape(128, 128)
+        bias = jnp.where((lane == 64) & (position >= length), jnp.full_like(block, -1e30), table)
+        k_ref[group, at_row : at_row + 128, :] = jnp.where(low_lane, block, bias)
+        v_ref[group, at_row : at_row + 128, :] = jnp.where(low_lane, jnp.ones_like(block), block)
+
+    def prepare_keys(e, turn):
         d = ARRIVAL[e]
-        sib_copies[d].wait_recv()
+        sib_copies[d, turn].wait_recv()
         for source, core_ in ((own, core), (sib, 1 - core)):
-            masked = (lane == 64) & (steps + start_of(half, slot(d), core_) >= length)
-            at_row = e * 512 + (0 if source is own else 256)
+            mine = source is own
             for group in range(3):
-                at_lane = TILE_OF[group] * 128 - (0 if source is own else 256)
-                block = source[d, :, :, at_lane : at_lane + 128].reshape(256, 128)
-                bias = jnp.where(masked, jnp.full_like(block, -1e30), k_tab[group])
-                k_op[group, at_row : at_row + 256, :] = jnp.where(low_lane, block, bias)
-                v_op[group, at_row : at_row + 256, :] = jnp.where(low_lane, jnp.ones_like(block), block)
-        for group in range(3):
-            at_lane = (group // 2) * 128
-            q = own[d, :, :, at_lane : at_lane + 128].reshape(256, 128)
-            if group == 1:
-                q = pltpu.roll(q.astype(F32), 64, 1).astype(BF)
-            q_op[group, e] = jnp.where(low_lane, q, q_tab[...])
+                at_tile = PAIRS[group] + (0 if turn == 0 else 12 if mine else 6)
+                at_row = (0 if turn == 0 else 1024) + e * 256 + (0 if mine else 128)
+                offset = 4 * (group % 2 if turn == 0 else 1 - group % 2)
+                position = steps + (start_of(half, slot(d), core_) + offset)
+                table = k_tab[group] if turn == 0 else jnp.zeros((128, 128), BF)
+                keys(k_op, v_op, group, at_row, source[d, at_tile : at_tile + 2], position, table)
 
     def prepare_cross(e):
         d = ARRIVAL[e]
         xs_copies[d].wait_recv()
         for source, core_ in ((x_own, core), (x_sib, 1 - core)):
-            at_row = e * 256 + (0 if source is x_own else 128)
             for group in range(3):
-                at_lane = TILE_OF[group] * 128 - 256
-                block = source[d, :, :, at_lane : at_lane + 128].reshape(128, 128)
-                position = steps[0:128] + start_of(1 - half, cross_slot(d), core_) + 4 * (group % 2)
-                masked = (lane[0:128] == 64) & (position >= length)
-                bias = jnp.where(masked, jnp.full_like(block, -1e30), x_tab[group])
-                xk_op[group, at_row : at_row + 128, :] = jnp.where(low_lane[0:128], block, bias)
-                xv_op[group, at_row : at_row + 128, :] = jnp.where(low_lane[0:128], jnp.ones_like(block), block)
+                at_row = e * 256 + (0 if source is x_own else 128)
+                position = steps + (start_of(1 - half, cross_slot(d), core_) + 4 * (group % 2))
+                block = source[d, PAIRS[group] : PAIRS[group] + 2]
+                keys(xk_op, xv_op, group, at_row, block, position, x_tab[group])
+
+    def prepare_queries(e):
+        d = ARRIVAL[e]
+        for pair in range(2):
+            both = own[d, 6 + 2 * pair : 8 + 2 * pair].reshape(128, 128)
+            packed = own[d, 10 + pair].astype(F32)
+            last = jnp.concatenate([packed, pltpu.roll(packed, 64, 1)], axis=0).astype(BF)
+            moved = pltpu.roll(both.astype(F32), 64, 1).astype(BF)
+            for group, q in enumerate((both, moved, last)):
+                begin = e * 256 + pair * 128
+                q_op[group, begin : begin + 128, :] = jnp.where(low_lane, q, q_tab[pair])
 
     contract = (((1,), (1,)), ((), ()))
 
-    def wide(column, count):
-        return jnp.concatenate([column] * count, axis=1)
-
-    def mix(q, keys, values, state):
-        scores = lax.dot_general(q, keys, contract, preferred_element_type=F32)
-        top = jnp.broadcast_to(jnp.max(scores, axis=1, keepdims=True), (q.shape[0], 128))
-        if state is not None:
-            top = jnp.maximum(state[0], top)
-        expo = jnp.exp(scores - wide(top, scores.shape[1] // 128)).astype(BF)
-        acc = jnp.dot(expo, values, preferred_element_type=F32)
-        if state is not None:
-            acc += state[1] * jnp.exp(state[0] - top)
-        return top, acc
-
-    def parts(group, todo):
-        states = [None if fresh else (tops[group, e], sums[group, e]) for e, _, _, fresh in todo]
-        found = [
-            mix(q_op[group, e], k_op[group, begin:end, :], v_op[group, begin:end, :], state)
-            for (e, begin, end, _), state in zip(todo, states)
-        ]
-        for (e, _, _, _), (top, acc) in zip(todo, found):
-            tops[group, e] = top
-            sums[group, e] = acc
-
-    def cross_parts(groups, begin, end):
-        todo = []
-        for group in groups:
-            rows = pl.ds(pl.multiple_of(128 * lax.rem(group, 2), 128), 128)
-            for both in ((0, 1), (2, 3)):
-                todo.append((group, rows, both))
-
-        def load(ref, group, rows, both):
-            return jnp.concatenate([ref[group, e, rows, :] for e in both], axis=0)
-
-        states = [(load(tops, *what), load(sums, *what)) for what in todo]
-        queries = [load(q_op, *what) for what in todo]
-        found = [
-            mix(q, xk_op[what[0], begin:end, :], xv_op[what[0], begin:end, :], state)
-            for what, q, state in zip(todo, queries, states)
-        ]
-        for (group, rows, both), (top, acc) in zip(todo, found):
-            for index, e in enumerate(both):
-                tops[group, e, rows, :] = top[index * 128 : index * 128 + 128]
-                sums[group, e, rows, :] = acc[index * 128 : index * 128 + 128]
-
-    arrive(0)
-    prepare(0)
+    def mix(q, k_ref, v_ref, group, begin, end, state):
+        for at_key in range(begin, end, 512):
+            span = pl.ds(at_key, 512)
+            scores = lax.dot_general(q, k_ref[group, span, :], contract, preferred_element_type=F32)
+            top = jnp.broadcast_to(jnp.max(scores, axis=1, keepdims=True), (q.shape[0], 128))
+            if state is not None:
+                top = jnp.maximum(state[0], top)
+            expo = jnp.exp(scores - jnp.concatenate([top] * 4, axis=1)).astype(BF)
+            acc = jnp.dot(expo, v_ref[group, span, :], preferred_element_type=F32)
+            if state is not None:
+                acc += state[1] * jnp.exp(state[0] - top)
+            state = (top, acc)
+        return state
+
+    def part(group, rows, begin, end, fresh):
+        state = None if fresh else (tops[group, rows, :], sums[group, rows, :])
+        return mix(q_op[group, rows, :], k_op, v_op, group, begin, end, state)
+
+    def keep(group, rows, state):
+        tops[group, rows, :], sums[group, rows, :] = state
+
+    share(0, 0)
+    share(0, 2)
+    prepare_queries(0)
+    for d in (2, 1):
+        third[d, 0].wait_send()
+        send(d, 1)
+    third[3, 0].wait_send()
+    send(3, 1)
+    for d in (2, 1, 3):
+        share(d, 0)
+    for e in range(4):
+        prepare_keys(e, 0)
+    share_cross(0)
+    found = [part(group, pl.ds(0, 256), 0, 1024, True) for group in range(3)]
     for group in range(3):
-        parts(group, [(0, 0, 512, True)])
-    arrive(2)
-    arrive(1)
-    prepare(1)
-    prepare(2)
-
-    @pl.loop(0, 3)
-    def _(group):
-        parts(group, [(0, 512, 1536, False), (1, 0, 1536, True), (2, 0, 1536, True)])
-
-    arrive(3)
-    for d in (0, 2, 1):
-        arrive_cross(d)
-    prepare(3)
-
-    @pl.loop(0, 3)
-    def _(group):
-        parts(group, [(3, 0, 2048, True)] + [(e, 1536, 2048, False) for e in range(3)])
-
-    def finish(group, e, begin):
-        acc = sums[group, e, begin : begin + 128, :]
-        position = steps[begin : begin + 128] + start_of(half, slot(ARRIVAL[e]), core)
+        keep(group, pl.ds(0, 256), found[group])
+    for d in (2, 1, 3):
+        send(d, 2)
+    for e in range(1, 4):
+        third[ARRIVAL[e], 1].wait_recv()
+        prepare_queries(e)
+
+    for group in range(3):
+        rows = pl.ds(256, 768)
+        keep(group, rows, part(group, rows, 0, 1024, True))
+
+    prepare_keys(0, 2)
+    for d in (2, 1, 3):
+        share(d, 2)
+    for d in (2, 1, 3):
+        share_cross(d)
+    for e in range(1, 4):
+        prepare_keys(e, 2)
+
+    for group in range(3):
+        rows = pl.ds(0, 1024)
+        keep(group, rows, part(group, rows, 1024, 2048, False))
+
+    def finish(group, e, pair):
+        acc = sums[group, e * 256 + pair * 128 : e * 256 + pair * 128 + 128, :]
+        position = steps + (start_of(half, slot(ARRIVAL[e]), core) + 4 * pair)
         return jnp.where(position < length, acc / pltpu.roll(acc, 64, 1), 0.0)
 
     outs = []
 
     def give(turn):
-        wide, narrow = (128, 0) if turn == 0 else (0, 128)
         for e in (3, 1, 2, 0):
             d = ARRIVAL[e]
-            low, high = finish(0, e, wide), finish(2, e, wide)
-            middle = finish(1, e, narrow)
-            joined = jnp.where(low_lane[0:128], pltpu.roll(low, 64, 1), high)
-            packed = jnp.where(low_lane[0:64], pltpu.roll(middle[0:64], 64, 1), middle[64:128])
+            low, high, middle = finish(0, e, 1 - turn), finish(2, e, 1 - turn), finish(1, e, turn)
+            joined = jnp.where(low_lane, pltpu.roll(low, 64, 1), high)
+            packed = jnp.where(low64, pltpu.roll(middle[0:64], 64, 1), middle[64:128])
             attn[d, 3 * turn : 3 * turn + 2] = joined.astype(BF).reshape(2, 64, 128)
             attn[d, 3 * turn + 2] = packed.astype(BF)
             src, dst = attn.at[d, pl.ds(3 * turn, 3)], back.at[cls, pl.ds(3 * turn, 3)]
@@ -406,25 +426,27 @@
             outs.append(copy)
 
     give(0)
-    arrive_cross(3)
-    for e in range(3):
+    for e in range(4):
         prepare_cross(e)
 
-    @pl.loop(0, 3)
-    def _(group):
-        cross_parts([group], 0, 768)
-
-    prepare_cross(3)
-    cross_parts(range(3), 768, 1024)
+    for group in range(3):
+        first = 128 * (group % 2)
+        rows = [pl.ds(e * 256 + first, 128) for e in range(4)]
+        q, top, acc = [jnp.concatenate([ref[group, r, :] for r in rows], axis=0) for ref in (q_op, tops, sums)]
+        top, acc = mix(q, xk_op, xv_op, group, 0, 1024, (top, acc))
+        for e in range(4):
+            sums[group, rows[e], :] = acc[e * 128 : e * 128 + 128]
+
     give(1)
     for copy in outs:
         copy.wait()
     for d in range(4):
         if d > 0:
-            first[d].wait_send()
-        sib_copies[d].wait_send()
-        for copy in x_copies[d]:
-            copy.wait_send()
+            third[d, 1].wait_send()
+            third[d, 2].wait_send()
+        sib_copies[d, 0].wait_send()
+        sib_copies[d, 2].wait_send()
+        x_copies[d].wait_send()
         xs_copies[d].wait_send()
 
 
@@ -437,28 +459,28 @@
         in_specs=[vmem, pl.BlockSpec(memory_space=pltpu.SMEM)],
         out_specs=pl.BlockSpec(memory_space=pltpu.HBM),
         scratch_shapes=[
-            pltpu.VMEM((4, 4, 64, WIDE), BF),
-            pltpu.VMEM((4, 4, 64, 384), BF),
-            pltpu.VMEM((4, 2, 64, 384), BF),
-            pltpu.VMEM((4, 2, 64, 384), BF),
-            pltpu.VMEM((3, 4, 64, WIDE), BF),
-            pltpu.VMEM((3, 4, 256, 128), BF),
+            pltpu.VMEM((4, 18, 64, 128), BF),
+            pltpu.VMEM((4, 12, 64, 128), BF),
+            pltpu.VMEM((4, 6, 64, 128), BF),
+            pltpu.VMEM((4, 6, 64, 128), BF),
+            pltpu.VMEM((3, 18, 64, 128), BF),
+            pltpu.VMEM((3, 1024, 128), BF),
             pltpu.VMEM((3, 2048, 128), BF),
             pltpu.VMEM((3, 2048, 128), BF),
             pltpu.VMEM((3, 1024, 128), BF),
             pltpu.VMEM((3, 1024, 128), BF),
-            pltpu.VMEM((3, 4, 256, 128), F32),
-            pltpu.VMEM((3, 4, 256, 128), F32),
+            pltpu.VMEM((3, 1024, 128), F32),
+            pltpu.VMEM((3, 1024, 128), F32),
             pltpu.VMEM((4, 6, 64, 128), BF),
-            pltpu.VMEM((256, 128), BF),
-            pltpu.VMEM((3, 256, 128), BF),
+            pltpu.VMEM((2, 128, 128), BF),
             pltpu.VMEM((3, 128, 128), BF),
-            dma((3,)),
-            dma((3,)),
+            pltpu.VMEM((3, 128, 128), BF),
+            dma((3, 3)),
+            dma((3, 3)),
+            dma((4, 2)),
+            dma((4, 2)),
             dma((4,)),
             dma((4,)),
-            dma((4, 2)),
-            dma((4, 2)),
             dma((4,)),
             dma((4,)),
             dma((2, 3)),

time: 78.2 us -> 69.8 us (0.89)
  Pallas kernels: 75.1 us -> 67.3 us
    pallas_call x1, Pallas kernels: 40.8 us -> 33 us  [attend(): pl.pallas_call(attend_kernel, out_shape=jax.ShapeDtypeStruct((4, 6, 64, 1...]
where the time goes in v3:
time: 69.8 us; the launch traced here: 69.6 us
  Pallas kernels  67.3 us (96%)
  local copies, waits for them, and re-layouts  2.26 us (3%)
    pallas_call x1, Pallas kernels, attend(): pl.pallas_call(attend_kernel, out_shape=jax.ShapeDtypeStruct((4, 6, 64, 1...  33 us
    pallas_call x1, Pallas kernels, project(): pl.pallas_call(project_kernel, out_shape=jax.ShapeDtypeStruct((DEVICES, B...  30 us
    pallas_call x1, Pallas kernels, output(): pl.pallas_call(output_kernel, grid=(4,), out_shape=jax.ShapeDtypeStruct((...  4.33 us
    unnamed x4, local copies, waits for them, and re-layouts  2.26 us

profile of v3, /device:TPU:1, one launch (start us, length us, event | category | flops | bytes accessed | tf_op | source)
XLA Modules:
  0.0 69.6 jit_solution(10528713793164550516)
XLA Ops:
  0.0 30.0 %project_send.1 = bf16[128,8,640]{2,1,0:T(8,128)(2,1)} custom-call(bf16[32,4,8,1536]{3,2,1,0:T(8,128)(2,1)} %bitcast.6, s32[8,128]{1,0:T(8,128)} %bitcast.7, bf16[1536,768]{1,0:T(8,128)(2,1)} %w_in.1, f32[6,128]{1,0:T(8,128)} %bitcast.8, bf16[768,2304]{1,0:T(8,128)(2,1)} %w_qkv.1), custom_call_target="tpu_custom_call" | custom-call | tf_op jit(solution)/shard_map/project_send/pallas_call | solution.py:144
  30.0 33.0 %attend.1.rows_in = bf16[4,6,64,128]{3,2,1,0:T(8,128)(2,1)} custom-call(bf16[1024,640]{1,0:T(8,128)(2,1)} %bitcast.5, s32[8]{0:T(128)} %valid.1), custom_call_target="tpu_custom_call" | custom-call | tf_op jit(solution)/shard_map/attend/pallas_call | solution.py:456
  63.0 0.0 copy-start
  63.0 1.0 %copy-done = bf16[4,6,64,128]{3,2,1,0:T(8,128)(2,1)S(1)} copy-done((bf16[4,6,64,128]{3,2,1,0:T(8,128)(2,1)S(1)}, bf16[4,6,64,128]{3,2,1,0:T(8,128)(2,1)}, u32[]{:S(2)}) %copy-start) | copy-done | bytes 393240
  64.0 0.0 copy-start.1
  64.0 1.3 %copy-done.1 = bf16[768,768]{1,0:T(8,128)(2,1)S(1)} copy-done((bf16[768,768]{1,0:T(8,128)(2,1)S(1)}, bf16[768,768]{1,0:T(8,128)(2,1)}, u32[]{:S(2)}) %copy-start.1) | copy-done | bytes 1179672
  65.3 4.3 %output.1 = bf16[1024,768]{1,0:T(8,128)(2,1)} custom-call(bf16[4,6,64,128]{3,2,1,0:T(8,128)(2,1)S(1)} %copy-done, bf16[768,768]{1,0:T(8,128)(2,1)S(1)} %copy-done.1), custom_call_target="tpu_custom_call" | custom-call | tf_op jit(solution)/shard_map/output/pallas_call | solution.py:518
Async XLA Ops:
  63.0 1.0 %copy-start = (bf16[4,6,64,128]{3,2,1,0:T(8,128)(2,1)S(1)}, bf16[4,6,64,128]{3,2,1,0:T(8,128)(2,1)}, u32[]{:S(2)}) copy-start(bf16[4,6,64,128]{3,2,1,0:T(8,128)(2,1)} %attend.1.rows_in) | copy-start | bytes 1179652
  64.0 1.3 %copy-start.1 = (bf16[768,768]{1,0:T(8,128)(2,1)S(1)}, bf16[768,768]{1,0:T(8,128)(2,1)}, u32[]{:S(2)}) copy-start(bf16[768,768]{1,0:T(8,128)(2,1)} %weight.1) | copy-start | bytes 3538948

commit v4 on v3

v4 whole, which is shorter than its diff:
```python
import functools

import jax
import jax.numpy as jnp
from jax import lax
from jax.experimental import pallas as pl
from jax.experimental.pallas import tpu as pltpu
from jax.sharding import PartitionSpec as P

MESH = pl.DeviceIdType.MESH
SLIDES = 8
SEQ = 16
DEVICES = 128
ROWS = 1024
BLOCK = 8
E = 1536
D = 768
WIDE = 640
PLACES = 4
VMEM_LIMIT = 63 * 1024 * 1024
BF = jnp.bfloat16
F32 = jnp.float32
I32 = jnp.int32


def iota(shape, dim):
    return lax.broadcasted_iota(I32, shape, dim)


def pick_columns(qkv, place):
    rows = qkv.shape[0]
    lane = iota((rows, 128), 1)
    cls = place & 3
    high = cls >= 2
    odd = (cls & 1) == 1
    low_lane = lane < 64

    def head(kind, group):
        at = kind * D + group * 256
        return jnp.where(high, qkv[:, at + 128 : at + 256], qkv[:, at : at + 128])

    def pair(left, right):
        moved = pltpu.roll(jnp.where(odd, left, right), 64, 1)
        return jnp.where(low_lane == odd, moved, jnp.where(odd, right, left))

    step = (place >> 2) & 3
    sorted_at = cls * 256 + (((step & 1) << 1) | (step >> 1)) * 64 + (place >> 4)
    ids = jnp.where(lane == 64, sorted_at >> 7, jnp.where(lane == 65, sorted_at & 127, 0)).astype(F32)
    q2 = head(0, 2) * 0.125
    q2 = jnp.where(odd, pltpu.roll(q2, 64, 1), q2)
    return (
        pair(head(0, 0) * 0.125, head(0, 1) * 0.125),
        jnp.where(low_lane, q2, ids),
        pair(head(1, 0), head(2, 0)),
        pair(head(1, 2), head(2, 2)),
        pair(head(1, 1), head(2, 1)),
    )


def project_kernel(tiles, dest, w_in, gain, w_qkv, recv, tiles_v, w_in_v, w_qkv_v, dest_v, gain_v, send, load_sem, send_sem, recv_sem, own_sem):
    slide = lax.axis_index("slide")
    seq = lax.axis_index("seq")
    me = slide * SEQ + seq
    across = seq // PLACES
    place_me = lax.rem(seq, PLACES)

    def place_at(step):
        return lax.rem(place_me + step, PLACES)

    loads = [
        pltpu.make_async_copy(w_in, w_in_v, load_sem.at[0]),
        pltpu.make_async_copy(w_qkv, w_qkv_v, load_sem.at[1]),
        pltpu.make_async_copy(dest, dest_v, load_sem.at[2]),
        pltpu.make_async_copy(gain, gain_v, load_sem.at[3]),
    ]
    for step in range(PLACES):
        loads.append(pltpu.make_async_copy(tiles.at[:, :, :, place_at(step)], tiles_v.at[step], load_sem.at[4 + step]))
    for index in (0, 4, 2, 3, 1, 5, 6, 7):
        loads[index].start()

    barrier = pltpu.get_barrier_semaphore()

    @pl.loop(1, DEVICES)
    def _(i):
        other = lax.rem(me + i, DEVICES)
        pl.semaphore_signal(barrier, inc=1, device_id=(other // SEQ, lax.rem(other, SEQ)), device_id_type=MESH)

    def wait_first(step, load):
        if step == 0:
            load.wait()

    for step in range(PLACES + 1):
        turn = max(step - 1, 0)
        place = place_at(turn)
        across_low = lax.rem(across + step, 2) if step < 2 else None
        blocks = DEVICES // PLACES // (2 if step < 2 else 1)
        rows = blocks * BLOCK
        wait_first(step, loads[0])
        if step != 1:
            loads[4 + turn].wait()
        x = tiles_v[turn, :, :, across_low] if step < 2 else tiles_v[turn]
        proj = jnp.dot(x.reshape(rows, E), w_in_v[...], preferred_element_type=F32).astype(BF).astype(F32)
        mean = jnp.mean(proj, axis=-1, keepdims=True)
        centred = proj - mean
        var = jnp.mean(centred * centred, axis=-1, keepdims=True)
        wait_first(step, loads[3])
        gains = jnp.concatenate([gain_v[i : i + 1, :] for i in range(D // 128)], axis=1)
        normed = (centred * lax.rsqrt(var + 1e-05) * gains).astype(BF)
        wait_first(step, loads[1])
        qkv = jnp.dot(normed, w_qkv_v[...], preferred_element_type=F32)
        wait_first(step, loads[2])
        lines = (dest_v[...] & (ROWS - 1)).astype(F32)
        lines = jnp.broadcast_to(lines.reshape(8, 1, 128), (8, rows // 8, 128)).reshape(rows, 128)
        r = iota((rows, 128), 0)
        to = (r >> 3) & 3 if step >= 2 else ((r >> 3) & 1) * 2 + across_low
        wanted = to * 32 + place * 8 + (r & 7)
        position = jnp.sum(jnp.where(iota((rows, 128), 1) == wanted, lines, 0.0), axis=1, keepdims=True).astype(I32)
        for index, block in enumerate(pick_columns(qkv, position)):
            lanes = pl.ds(index * 128, 128)
            if step < 2:
                send[:, :, across_low, place, :, lanes] = block.reshape(SLIDES, 2, BLOCK, 128).astype(BF)
            else:
                send[:, :, :, place, :, lanes] = block.reshape(SLIDES, 2, 2, BLOCK, 128).astype(BF)
        if step == 0:
            pl.semaphore_wait(barrier, DEVICES - 1)

        @pl.loop(0, blocks)
        def _(i):
            to_slide = lax.rem(slide + i, SLIDES)
            to_across = lax.rem(across + (i // SLIDES * 2 + step if step < 2 else i // SLIDES), 4)

            @pl.when((to_slide != slide) | (to_across != across) | (place != place_me))
            def _():
                pltpu.make_async_remote_copy(
                    src_ref=send.at[to_slide, to_across // 2, lax.rem(to_across, 2), place],
                    dst_ref=recv.at[me],
                    send_sem=send_sem,
                    recv_sem=recv_sem,
                    device_id=(to_slide, to_across * PLACES + place),
                    device_id_type=MESH,
                ).start()

    own = pltpu.make_async_copy(send.at[slide, across // 2, lax.rem(across, 2), place_me], recv.at[me], own_sem)
    own.start()
    own.wait()
    rest = pl.ds(0, DEVICES - 1)
    pltpu.make_async_copy(recv.at[rest], recv.at[rest], send_sem).wait()
    pltpu.make_async_copy(recv.at[rest], recv.at[rest], recv_sem).wait()


def project(tiles, dest, w_in, gain, w_qkv):
    hbm = pl.BlockSpec(memory_space=pltpu.HBM)
    return pl.pallas_call(
        project_kernel,
        out_shape=jax.ShapeDtypeStruct((DEVICES, BLOCK, WIDE), BF),
        in_specs=[hbm] * 5,
        out_specs=hbm,
        scratch_shapes=[
            pltpu.VMEM((PLACES, SLIDES, 2, 2, BLOCK, E), BF),
            pltpu.VMEM((E, D), BF),
            pltpu.VMEM((D, 3 * D), BF),
            pltpu.VMEM((8, 128), I32),
            pltpu.VMEM((D // 128, 128), F32),
            pltpu.VMEM((SLIDES, 2, 2, PLACES, BLOCK, WIDE), BF),
            pltpu.SemaphoreType.DMA((4 + PLACES,)),
            pltpu.SemaphoreType.DMA,
            pltpu.SemaphoreType.DMA,
            pltpu.SemaphoreType.DMA,
        ],
        compiler_params=pltpu.CompilerParams(collective_id=0, has_side_effects=True, vmem_limit_bytes=VMEM_LIMIT),
        name="project_send",
    )(tiles, dest, w_in, gain, w_qkv)


ARRIVAL = (0, 2, 1, 3)
PAIR_OF = ((0, 1), (2, 3), (1, 0))
LN2 = (0.69140625, 0.0017409306)
LN3 = (1.1015625, -0.0029502113)
KV_AT = (2, 4, 3)


def key_table(group, inner):
    lane = iota((128, 128), 1)
    key = iota((128, 128), 0) // 64 + 2 * (group % 2)
    third, second = PAIR_OF[group]
    query = jnp.where(lane < 69, lane - 65, lane - 69)
    used = (lane >= 65) & (lane < 73)
    twice = used & ((query == third) | (query == second))
    thrice = used & (query == third) & (key == third)
    first = lane < 69
    ln2 = jnp.where(first, LN2[0], LN2[1])
    ln3 = jnp.where(first, LN3[0], LN3[1])
    if inner:
        return jnp.where(thrice, ln3, jnp.where(twice, ln2, 0.0))
    return jnp.where(thrice, ln2, 0.0)


def attend_kernel(
    recv, valid, back, own, sib, x_own, x_sib, stage, q_op, k_op, v_op, xk_op, xv_op, tops, sums, attn, q_tab, k_tab, x_tab,
    send_sem, recv_sem, sib_send, sib_recv, x_send, x_recv, xs_send, xs_recv, out_send, out_recv, own_sem,
):
    slide = lax.axis_index("slide")
    seq = lax.axis_index("seq")
    half = seq // 8
    row = lax.rem(seq // 4, 2)
    col = lax.rem(seq // 2, 2)
    core = lax.rem(seq, 2)

    def slot(d):
        return 2 * lax.rem(row + d // 2, 2) + lax.rem(col + d % 2, 2)

    def cross_slot(d):
        return 2 * lax.rem(1 - row + d // 2, 2) + lax.rem(col + d % 2, 2)

    def cls_of(d):
        return 2 * lax.rem(row + d // 2 + half, 2) + lax.rem(col + d % 2, 2)

    def device(d):
        return (slide, half * 8 + slot(d) * 2 + core)

    sibling = (slide, seq + 1 - 2 * core)
    cross = (slide, (1 - half) * 8 + cross_slot(0) * 2 + core)
    partners = [device(1), device(2), device(3), sibling, cross]

    barrier = pltpu.get_barrier_semaphore()
    for other in partners:
        pl.semaphore_signal(barrier, inc=1, device_id=other, device_id_type=MESH)

    rows_in = recv[...]
    lane8 = iota((8, 128), 1)
    weigh = jnp.where(lane8 == 64, 128.0, jnp.where(lane8 == 65, 1.0, 0.0)).astype(BF)
    at = lax.dot_general(weigh, rows_in[:, 128:256], (((1,), (1,)), ((), ())), preferred_element_type=F32)
    at = at[0:1].astype(I32)
    low64 = iota((64, 128), 1) < 64

    def sort_class(cls, ref):
        hit = (at - cls * 256) == iota((256, ROWS), 0)
        one_hot = jnp.where(hit, 1.0, 0.0).astype(BF)
        found = jnp.dot(one_hot, rows_in, preferred_element_type=F32)

        def tile(a, t):
            return found[a * 64 : a * 64 + 64, t * 128 : t * 128 + 128]

        for group in range(3):
            for i in range(4):
                ref[6 * group + i] = tile((2 * (group % 2) + i) % 4, KV_AT[group]).astype(BF)
            for pair in range(2):
                even, odd = tile(2 * pair, group // 2), tile(2 * pair + 1, group // 2)
                if group == 1:
                    even = pltpu.roll(even, 64, 1)
                else:
                    odd = pltpu.roll(odd, 64, 1)
                ref[6 * group + 4 + pair] = jnp.where(low64, even, odd).astype(BF)

    def remote(src, dst, send, recv_, to):
        return pltpu.make_async_remote_copy(
            src_ref=src, dst_ref=dst, send_sem=send, recv_sem=recv_, device_id=to, device_id_type=MESH
        )

    sends = {}

    def send(d, group):
        part = pl.ds(6 * group, 6)
        copy = remote(
            stage.at[d - 1, part], own.at[d, part], send_sem.at[d - 1, group], recv_sem.at[d - 1, group], device(d)
        )
        copy.start()
        sends[d, group] = copy

    for order, d in enumerate(ARRIVAL[1:]):
        sort_class(cls_of(d), stage.at[d - 1])
        if order == 0:
            pl.semaphore_wait(barrier, len(partners))
        send(d, 0)
    for group in range(1, 3):
        for d in ARRIVAL[1:]:
            send(d, group)
    sort_class(cls_of(0), own.at[0])

    sib_copies, x_copies, xs_copies = {}, {}, {}

    def share(d, group):
        if d > 0:
            sends[d, group].wait_recv()
        sib_copies[d, group] = remote(
            own.at[d, pl.ds(6 * group, 4)], sib.at[d, pl.ds(4 * group, 4)], sib_send.at[d, group], sib_recv.at[d, group], sibling
        )
        sib_copies[d, group].start()
        x_copies[d, group] = remote(
            own.at[d, pl.ds(6 * group, 2)], x_own.at[d, pl.ds(2 * group, 2)], x_send.at[d, group], x_recv.at[d, group], cross
        )
        x_copies[d, group].start()

    def share_cross(d, group):
        x_copies[d, group].wait_recv()
        part = pl.ds(2 * group, 2)
        xs_copies[d, group] = remote(x_own.at[d, part], x_sib.at[d, part], xs_send.at[d, group], xs_recv.at[d, group], sibling)
        xs_copies[d, group].start()

    cls = cls_of(0)
    length = valid[slide]
    lane = iota((128, 128), 1)
    low_lane = lane < 64
    line = iota((128, 128), 0)
    steps = lax.rem(line, 64) * 16 + (line // 64) * 8

    def start_of(half_, slot_, core_):
        return half_ * 8192 + slot_ * 2048 + core_ * 1024 + cls

    for pair in range(2):
        residue = line // 64 + 2 * pair
        ones = jnp.where((lane == 64) | (lane == 65 + residue) | (lane == 69 + residue), 1.0, 0.0)
        q_tab[pair] = ones.astype(BF)
    for group in range(3):
        k_tab[group] = key_table(group, True).astype(BF)
        x_tab[group] = key_table(group, False).astype(BF)

    def keys(k_ref, v_ref, group, at_row, block, position, table):
        block = block.reshape(128, 128)
        bias = jnp.where((lane == 64) & (position >= length), jnp.full_like(block, -1e30), table)
        k_ref[group, at_row : at_row + 128, :] = jnp.where(low_lane, block, bias)
        v_ref[group, at_row : at_row + 128, :] = jnp.where(low_lane, jnp.ones_like(block), block)

    def prepare(e, group):
        d = ARRIVAL[e]
        for pair in range(2):
            packed = own[d, 6 * group + 4 + pair].astype(F32)
            q = jnp.concatenate([packed, pltpu.roll(packed, 64, 1)], axis=0).astype(BF)
            begin = e * 256 + pair * 128
            q_op[group, begin : begin + 128, :] = jnp.where(low_lane, q, q_tab[pair])
        sib_copies[d, group].wait_recv()
        for source, core_, first in ((own, core, 6 * group), (sib, 1 - core, 4 * group)):
            for rest in range(2):
                at_row = e * 512 + rest * 256 + (0 if source is own else 128)
                position = steps + (start_of(half, slot(d), core_) + 4 * ((group + rest) % 2))
                table = k_tab[group] if rest == 0 else jnp.zeros((128, 128), BF)
                at_tile = first + 2 * rest
                keys(k_op, v_op, group, at_row, source[d, at_tile : at_tile + 2], position, table)

    def prepare_cross(e, group):
        d = ARRIVAL[e]
        xs_copies[d, group].wait_recv()
        for source, core_ in ((x_own, core), (x_sib, 1 - core)):
            at_row = e * 256 + (0 if source is x_own else 128)
            position = steps + (start_of(1 - half, cross_slot(d), core_) + 4 * (group % 2))
            keys(xk_op, xv_op, group, at_row, source[d, 2 * group : 2 * group + 2], position, x_tab[group])

    contract = (((1,), (1,)), ((), ()))

    def mix(q, k_ref, v_ref, group, spans, state):
        for begin, end in spans:
            span = pl.ds(begin, end - begin)
            scores = lax.dot_general(q, k_ref[group, span, :], contract, preferred_element_type=F32)
            top = jnp.broadcast_to(jnp.max(scores, axis=1, keepdims=True), (q.shape[0], 128))
            if state is not None:
                top = jnp.maximum(state[0], top)
            expo = jnp.exp(scores - jnp.concatenate([top] * ((end - begin) // 128), axis=1)).astype(BF)
            acc = jnp.dot(expo, v_ref[group, span, :], preferred_element_type=F32)
            if state is not None:
                acc += state[1] * jnp.exp(state[0] - top)
            state = (top, acc)
        return state

    outs = []

    def give(e, group):
        d = ARRIVAL[e]
        for pair in range(2):
            acc = sums[group, e * 256 + pair * 128 : e * 256 + pair * 128 + 128, :]
            position = steps + (start_of(half, slot(d), core) + 4 * pair)
            out = jnp.where(position < length, acc / pltpu.roll(acc, 64, 1), 0.0)
            attn[d, 2 * group + pair] = jnp.where(low64, pltpu.roll(out[0:64], 64, 1), out[64:128]).astype(BF)
        part = pl.ds(2 * group, 2)
        src, dst = attn.at[d, part], back.at[cls, part]
        if d > 0:
            copy = remote(src, dst, out_send.at[group, d - 1], out_recv.at[group, d - 1], device(d))
        else:
            copy = pltpu.make_async_copy(src, dst, own_sem.at[group])
        copy.start()
        outs.append(copy)

    def attend_half(group):
        for e in range(4):
            prepare(e, group)
        spans = [(begin, begin + 512) for begin in range(0, 2048, 512)]
        tops[group], sums[group] = mix(q_op[group], k_op, v_op, group, spans, None)

    def attend_cross(group):
        for e in range(4):
            prepare_cross(e, group)
        first = 128 * (group % 2)
        rows = [pl.ds(e * 256 + first, 128) for e in range(4)]
        q, top, acc = [jnp.concatenate([ref[group, r, :] for r in rows], axis=0) for ref in (q_op, tops, sums)]
        _, acc = mix(q, xk_op, xv_op, group, ((0, 512), (512, 1024)), (top, acc))
        for e in range(4):
            sums[group, rows[e], :] = acc[e * 128 : e * 128 + 128]
        for e in (3, 1, 2, 0):
            give(e, group)

    for group in range(3):
        share(0, group)
    for d in ARRIVAL[1:]:
        share(d, 0)
    attend_half(0)
    for d in ARRIVAL[1:]:
        share(d, 1)
    for d in ARRIVAL:
        share_cross(d, 0)
    attend_half(1)
    for d in ARRIVAL[1:]:
        share(d, 2)
    for d in ARRIVAL:
        share_cross(d, 1)
    attend_cross(0)
    attend_half(2)
    for d in ARRIVAL:
        share_cross(d, 2)
    attend_cross(1)
    attend_cross(2)
    for copy in outs:
        copy.wait()
    for group in range(3):
        for d in range(4):
            if d > 0:
                sends[d, group].wait_send()
            sib_copies[d, group].wait_send()
            x_copies[d, group].wait_send()
            xs_copies[d, group].wait_send()


def attend(recv, valid):
    vmem = pl.BlockSpec(memory_space=pltpu.VMEM)
    dma = pltpu.SemaphoreType.DMA
    return pl.pallas_call(
        attend_kernel,
        out_shape=jax.ShapeDtypeStruct((4, 6, 64, 128), BF),
        in_specs=[vmem, pl.BlockSpec(memory_space=pltpu.SMEM)],
        out_specs=pl.BlockSpec(memory_space=pltpu.HBM),
        scratch_shapes=[
            pltpu.VMEM((4, 18, 64, 128), BF),
            pltpu.VMEM((4, 12, 64, 128), BF),
            pltpu.VMEM((4, 6, 64, 128), BF),
            pltpu.VMEM((4, 6, 64, 128), BF),
            pltpu.VMEM((3, 18, 64, 128), BF),
            pltpu.VMEM((3, 1024, 128), BF),
            pltpu.VMEM((3, 2048, 128), BF),
            pltpu.VMEM((3, 2048, 128), BF),
            pltpu.VMEM((3, 1024, 128), BF),
            pltpu.VMEM((3, 1024, 128), BF),
            pltpu.VMEM((3, 1024, 128), F32),
            pltpu.VMEM((3, 1024, 128), F32),
            pltpu.VMEM((4, 6, 64, 128), BF),
            pltpu.VMEM((2, 128, 128), BF),
            pltpu.VMEM((3, 128, 128), BF),
            pltpu.VMEM((3, 128, 128), BF),
            dma((3, 3)),
            dma((3, 3)),
            dma((4, 3)),
            dma((4, 3)),
            dma((4, 3)),
            dma((4, 3)),
            dma((4, 3)),
            dma((4, 3)),
            dma((3, 3)),
            dma((3, 3)),
            dma((3,)),
        ],
        compiler_params=pltpu.CompilerParams(collective_id=1, has_side_effects=True, vmem_limit_bytes=VMEM_LIMIT),
        name="attend",
    )(recv, valid)


def output_kernel(rows_hbm, weight_hbm, out, rows_in, weight, spread, packed, load_sem, out_sem):
    loads = [
        pltpu.make_async_copy(weight_hbm, weight, load_sem.at[0]),
        pltpu.make_async_copy(rows_hbm, rows_in, load_sem.at[1]),
    ]
    for copy in loads:
        copy.start()
    for copy in loads:
        copy.wait()
    low = iota((64, 128), 1) < 64
    for cls in range(4):
        heads = [weight[(cls + 4 * g) * 64 : (cls + 4 * g + 1) * 64, :] for g in range(3)]
        wide = jnp.concatenate([w for w in heads for _ in range(2)], axis=0)
        columns = []
        for g in range(3):
            tiles = [rows_in[cls, 2 * g + a // 2] for a in range(4)]
            masked = [jnp.where(low == (a % 2 == 0), tile, jnp.zeros_like(tile)) for a, tile in enumerate(tiles)]
            columns.append(jnp.concatenate(masked, axis=0))
        rows = jnp.concatenate(columns, axis=1)
        total = jnp.dot(rows, wide, preferred_element_type=F32)
        for a in range(4):
            residue = cls + (a % 2) * 8 + (a // 2) * 4
            for t in range(D // 128):
                spread[t, pl.ds(residue, 64, stride=16), :] = total[a * 64 : a * 64 + 64, t * 128 : t * 128 + 128]
    copies = []
    for index in range(4):
        span = pl.ds(index * 256, 256)
        for t in range(D // 128):
            packed[span, t * 128 : t * 128 + 128] = spread[t, span, :].astype(BF)
        copy = pltpu.make_async_copy(packed.at[span], out.at[span], out_sem.at[index])
        copy.start()
        copies.append(copy)
    for copy in copies:
        copy.wait()


def output(rows_in, weight):
    hbm = pl.BlockSpec(memory_space=pltpu.HBM)
    return pl.pallas_call(
        output_kernel,
        out_shape=jax.ShapeDtypeStruct((ROWS, D), BF),
        in_specs=[hbm, hbm],
        out_specs=hbm,
        scratch_shapes=[
            pltpu.VMEM((4, 6, 64, 128), BF),
            pltpu.VMEM((D, D), BF),
            pltpu.VMEM((D // 128, ROWS, 128), F32),
            pltpu.VMEM((ROWS, D), BF),
            pltpu.SemaphoreType.DMA((2,)),
            pltpu.SemaphoreType.DMA((4,)),
        ],
        compiler_params=pltpu.CompilerParams(vmem_limit_bytes=VMEM_LIMIT),
        name="output",
    )(rows_in, weight)


def local(tiles, destination, valid_len, in_weight, norm_gain, qkv_weight, out_weight):
    recv = project(tiles.reshape(SLIDES, 2, 2, PLACES, BLOCK, E), destination.reshape(8, 128), in_weight, norm_gain.reshape(D // 128, 128), qkv_weight)
    back = attend(recv.reshape(ROWS, WIDE), valid_len)
    return output(back, out_weight).reshape(1, ROWS, D)


def solution(mesh):
    in_specs = (P(("slide", "seq"), None), P(("slide", "seq")), P(), P(), P(), P(), P())
    return jax.shard_map(local, mesh=mesh, in_specs=in_specs, out_specs=P("slide", "seq", None), check_vma=False)
```

time: 69.8 us -> 67.2 us (0.963)
  local copies, waits for them, and re-layouts: 2.26 us -> 0 us
    unnamed x4 -> x0, local copies, waits for them, and re-layouts: 2.26 us -> none
where the time goes in v4:
time: 67.2 us; the launch traced here: 67 us
  Pallas kernels  66.8 us (99%)
    pallas_call x1, Pallas kernels, attend(): pl.pallas_call(attend_kernel, out_shape=jax.ShapeDtypeStruct((4, 6, 64, 1...  32.4 us
    pallas_call x1, Pallas kernels, project(): pl.pallas_call(project_kernel, out_shape=jax.ShapeDtypeStruct((DEVICES, B...  29.9 us
    pallas_call x1, Pallas kernels, output(): pl.pallas_call(output_kernel, out_shape=jax.ShapeDtypeStruct((ROWS, D), B...  4.54 us

profile of v4, /device:TPU:1, one launch (start us, length us, event | category | flops | bytes accessed | tf_op | source)
XLA Modules:
  0.0 67.0 jit_solution(2576039425617753957)
XLA Ops:
  0.0 29.9 %project_send.1 = bf16[128,8,640]{2,1,0:T(8,128)(2,1)} custom-call(bf16[8,2,2,4,8,1536]{5,4,3,2,1,0:T(8,128)(2,1)} %bitcast.6, s32[8,128]{1,0:T(8,128)} %bitcast.7, bf16[1536,768]{1,0:T(8,128)(2,1)} %w_in.1, f32[6,128]{1,0:T(8,128)} %bitcast.8, bf16[768,2304]{1,0:T(8,128)(2,1)} %w_qkv.1), custom_call_target="tpu_custom_call" | custom-call | tf_op jit(solution)/shard_map/project_send/pallas_call | solution.py:153
  29.9 32.4 %attend.1.rows_hbm = bf16[4,6,64,128]{3,2,1,0:T(8,128)(2,1)} custom-call(bf16[1024,640]{1,0:T(8,128)(2,1)} %bitcast.5, s32[8]{0:T(128)} %valid.1), custom_call_target="tpu_custom_call" | custom-call | tf_op jit(solution)/shard_map/attend/pallas_call | solution.py:434
  62.3 4.5 %output.1 = bf16[1024,768]{1,0:T(8,128)(2,1)} custom-call(bf16[4,6,64,128]{3,2,1,0:T(8,128)(2,1)} %attend.1.rows_hbm, bf16[768,768]{1,0:T(8,128)(2,1)} %weight_hbm.1), custom_call_target="tpu_custom_call" | custom-call | tf_op jit(solution)/shard_map/output/pallas_call | solution.py:511

commit v5 on v4

--- a/solution.py
+++ b/solution.py
@@ -15,8 +15,8 @@
 BLOCK = 8
 E = 1536
 D = 768
-WIDE = 640
 PLACES = 4
+CHUNK = 256
 VMEM_LIMIT = 63 * 1024 * 1024
 BF = jnp.bfloat16
 F32 = jnp.float32
@@ -27,157 +27,39 @@
     return lax.broadcasted_iota(I32, shape, dim)
 
 
-def pick_columns(qkv, place):
-    rows = qkv.shape[0]
+WIDTHS = (256, 256, 128)
+NEEDS = (((1, 0), (2, 0), (0, 0)), ((1, 1), (2, 1), (0, 1), (0, 2)), ((1, 2), (2, 2)))
+
+
+def pick_columns(turn, columns, place):
+    rows = place.shape[0]
     lane = iota((rows, 128), 1)
     cls = place & 3
     high = cls >= 2
     odd = (cls & 1) == 1
     low_lane = lane < 64
-
-    def head(kind, group):
-        at = kind * D + group * 256
-        return jnp.where(high, qkv[:, at + 128 : at + 256], qkv[:, at : at + 128])
+    heads = [jnp.where(high, block[:, 128:256], block[:, 0:128]) for block in columns]
 
     def pair(left, right):
         moved = pltpu.roll(jnp.where(odd, left, right), 64, 1)
         return jnp.where(low_lane == odd, moved, jnp.where(odd, right, left))
 
-    step = (place >> 2) & 3
-    sorted_at = cls * 256 + (((step & 1) << 1) | (step >> 1)) * 64 + (place >> 4)
-    ids = jnp.where(lane == 64, sorted_at >> 7, jnp.where(lane == 65, sorted_at & 127, 0)).astype(F32)
-    q2 = head(0, 2) * 0.125
-    q2 = jnp.where(odd, pltpu.roll(q2, 64, 1), q2)
-    return (
-        pair(head(0, 0) * 0.125, head(0, 1) * 0.125),
-        jnp.where(low_lane, q2, ids),
-        pair(head(1, 0), head(2, 0)),
-        pair(head(1, 2), head(2, 2)),
-        pair(head(1, 1), head(2, 1)),
-    )
-
-
-def project_kernel(tiles, dest, w_in, gain, w_qkv, recv, tiles_v, w_in_v, w_qkv_v, dest_v, gain_v, send, load_sem, send_sem, recv_sem, own_sem):
-    slide = lax.axis_index("slide")
-    seq = lax.axis_index("seq")
-    me = slide * SEQ + seq
-    across = seq // PLACES
-    place_me = lax.rem(seq, PLACES)
-
-    def place_at(step):
-        return lax.rem(place_me + step, PLACES)
-
-    loads = [
-        pltpu.make_async_copy(w_in, w_in_v, load_sem.at[0]),
-        pltpu.make_async_copy(w_qkv, w_qkv_v, load_sem.at[1]),
-        pltpu.make_async_copy(dest, dest_v, load_sem.at[2]),
-        pltpu.make_async_copy(gain, gain_v, load_sem.at[3]),
-    ]
-    for step in range(PLACES):
-        loads.append(pltpu.make_async_copy(tiles.at[:, :, :, place_at(step)], tiles_v.at[step], load_sem.at[4 + step]))
-    for index in (0, 4, 2, 3, 1, 5, 6, 7):
-        loads[index].start()
-
-    barrier = pltpu.get_barrier_semaphore()
-
-    @pl.loop(1, DEVICES)
-    def _(i):
-        other = lax.rem(me + i, DEVICES)
-        pl.semaphore_signal(barrier, inc=1, device_id=(other // SEQ, lax.rem(other, SEQ)), device_id_type=MESH)
-
-    def wait_first(step, load):
-        if step == 0:
-            load.wait()
-
-    for step in range(PLACES + 1):
-        turn = max(step - 1, 0)
-        place = place_at(turn)
-        across_low = lax.rem(across + step, 2) if step < 2 else None
-        blocks = DEVICES // PLACES // (2 if step < 2 else 1)
-        rows = blocks * BLOCK
-        wait_first(step, loads[0])
-        if step != 1:
-            loads[4 + turn].wait()
-        x = tiles_v[turn, :, :, across_low] if step < 2 else tiles_v[turn]
-        proj = jnp.dot(x.reshape(rows, E), w_in_v[...], preferred_element_type=F32).astype(BF).astype(F32)
-        mean = jnp.mean(proj, axis=-1, keepdims=True)
-        centred = proj - mean
-        var = jnp.mean(centred * centred, axis=-1, keepdims=True)
-        wait_first(step, loads[3])
-        gains = jnp.concatenate([gain_v[i : i + 1, :] for i in range(D // 128)], axis=1)
-        normed = (centred * lax.rsqrt(var + 1e-05) * gains).astype(BF)
-        wait_first(step, loads[1])
-        qkv = jnp.dot(normed, w_qkv_v[...], preferred_element_type=F32)
-        wait_first(step, loads[2])
-        lines = (dest_v[...] & (ROWS - 1)).astype(F32)
-        lines = jnp.broadcast_to(lines.reshape(8, 1, 128), (8, rows // 8, 128)).reshape(rows, 128)
-        r = iota((rows, 128), 0)
-        to = (r >> 3) & 3 if step >= 2 else ((r >> 3) & 1) * 2 + across_low
-        wanted = to * 32 + place * 8 + (r & 7)
-        position = jnp.sum(jnp.where(iota((rows, 128), 1) == wanted, lines, 0.0), axis=1, keepdims=True).astype(I32)
-        for index, block in enumerate(pick_columns(qkv, position)):
-            lanes = pl.ds(index * 128, 128)
-            if step < 2:
-                send[:, :, across_low, place, :, lanes] = block.reshape(SLIDES, 2, BLOCK, 128).astype(BF)
-            else:
-                send[:, :, :, place, :, lanes] = block.reshape(SLIDES, 2, 2, BLOCK, 128).astype(BF)
-        if step == 0:
-            pl.semaphore_wait(barrier, DEVICES - 1)
-
-        @pl.loop(0, blocks)
-        def _(i):
-            to_slide = lax.rem(slide + i, SLIDES)
-            to_across = lax.rem(across + (i // SLIDES * 2 + step if step < 2 else i // SLIDES), 4)
-
-            @pl.when((to_slide != slide) | (to_across != across) | (place != place_me))
-            def _():
-                pltpu.make_async_remote_copy(
-                    src_ref=send.at[to_slide, to_across // 2, lax.rem(to_across, 2), place],
-                    dst_ref=recv.at[me],
-                    send_sem=send_sem,
-                    recv_sem=recv_sem,
-                    device_id=(to_slide, to_across * PLACES + place),
-                    device_id_type=MESH,
-                ).start()
-
-    own = pltpu.make_async_copy(send.at[slide, across // 2, lax.rem(across, 2), place_me], recv.at[me], own_sem)
-    own.start()
-    own.wait()
-    rest = pl.ds(0, DEVICES - 1)
-    pltpu.make_async_copy(recv.at[rest], recv.at[rest], send_sem).wait()
-    pltpu.make_async_copy(recv.at[rest], recv.at[rest], recv_sem).wait()
-
-
-def project(tiles, dest, w_in, gain, w_qkv):
-    hbm = pl.BlockSpec(memory_space=pltpu.HBM)
-    return pl.pallas_call(
-        project_kernel,
-        out_shape=jax.ShapeDtypeStruct((DEVICES, BLOCK, WIDE), BF),
-        in_specs=[hbm] * 5,
-        out_specs=hbm,
-        scratch_shapes=[
-            pltpu.VMEM((PLACES, SLIDES, 2, 2, BLOCK, E), BF),
-            pltpu.VMEM((E, D), BF),
-            pltpu.VMEM((D, 3 * D), BF),
-            pltpu.VMEM((8, 128), I32),
-            pltpu.VMEM((D // 128, 128), F32),
-            pltpu.VMEM((SLIDES, 2, 2, PLACES, BLOCK, WIDE), BF),
-            pltpu.SemaphoreType.DMA((4 + PLACES,)),
-            pltpu.SemaphoreType.DMA,
-            pltpu.SemaphoreType.DMA,
-            pltpu.SemaphoreType.DMA,
-        ],
-        compiler_params=pltpu.CompilerParams(collective_id=0, has_side_effects=True, vmem_limit_bytes=VMEM_LIMIT),
-        name="project_send",
-    )(tiles, dest, w_in, gain, w_qkv)
+    picked = [pair(heads[0], heads[1])]
+    if turn == 0:
+        step = (place >> 2) & 3
+        sorted_at = cls * 256 + (((step & 1) << 1) | (step >> 1)) * 64 + (place >> 4)
+        ids = jnp.where(lane == 64, sorted_at >> 7, jnp.where(lane == 65, sorted_at & 127, 0)).astype(F32)
+        q = heads[2] * 0.125
+        picked.append(jnp.where(low_lane, jnp.where(odd, pltpu.roll(q, 64, 1), q), ids))
+    if turn == 1:
+        picked.append(pair(heads[2] * 0.125, heads[3] * 0.125))
+    return picked
 
 
 ARRIVAL = (0, 2, 1, 3)
 PAIR_OF = ((0, 1), (2, 3), (1, 0))
 LN2 = (0.69140625, 0.0017409306)
 LN3 = (1.1015625, -0.0029502113)
-KV_AT = (2, 4, 3)
-
 
 def key_table(group, inner):
     lane = iota((128, 128), 1)
@@ -195,16 +77,109 @@
     return jnp.where(thrice, ln2, 0.0)
 
 
-def attend_kernel(
-    recv, valid, back, own, sib, x_own, x_sib, stage, q_op, k_op, v_op, xk_op, xv_op, tops, sums, attn, q_tab, k_tab, x_tab,
+def layer_kernel(
+    tiles, dest, w_in, gain, w_qkv, valid, back,
+    tiles_v, w_in_v, w_qkv_v, dest_v, gain_v, normed_v, out0, out1, out2, in0, in1, in2, hot,
+    own, sib, x_own, x_sib, stage, q_op, k_op, v_op, xk_op, xv_op, tops, sums, attn, q_tab, k_tab, x_tab,
+    load_sem, go_sem, come_sem, stay_sem,
     send_sem, recv_sem, sib_send, sib_recv, x_send, x_recv, xs_send, xs_recv, out_send, out_recv, own_sem,
 ):
     slide = lax.axis_index("slide")
     seq = lax.axis_index("seq")
+    me = slide * SEQ + seq
+    across = seq // PLACES
+    place_me = lax.rem(seq, PLACES)
     half = seq // 8
     row = lax.rem(seq // 4, 2)
     col = lax.rem(seq // 2, 2)
     core = lax.rem(seq, 2)
+    leaving, coming = (out0, out1, out2), (in0, in1, in2)
+
+    def place_at(step):
+        return lax.rem(place_me + step, PLACES)
+
+    loads = [
+        pltpu.make_async_copy(w_in, w_in_v, load_sem.at[0]),
+        pltpu.make_async_copy(w_qkv, w_qkv_v, load_sem.at[1]),
+        pltpu.make_async_copy(dest, dest_v, load_sem.at[2]),
+        pltpu.make_async_copy(gain, gain_v, load_sem.at[3]),
+    ]
+    for step in range(PLACES):
+        loads.append(pltpu.make_async_copy(tiles.at[:, place_at(step)], tiles_v.at[step], load_sem.at[4 + step]))
+    for index in (0, 4, 2, 3, 1, 5, 6, 7):
+        loads[index].start()
+
+    barrier = pltpu.get_barrier_semaphore()
+
+    @pl.loop(1, DEVICES)
+    def _(i):
+        other = lax.rem(me + i, DEVICES)
+        pl.semaphore_signal(barrier, inc=1, device_id=(other // SEQ, lax.rem(other, SEQ)), device_id_type=MESH)
+
+    def project(step):
+        if step == 0:
+            loads[0].wait()
+            loads[3].wait()
+        loads[4 + step].wait()
+        x = tiles_v[step].reshape(CHUNK, E)
+        proj = jnp.dot(x, w_in_v[...], preferred_element_type=F32).astype(BF).astype(F32)
+        mean = jnp.mean(proj, axis=-1, keepdims=True)
+        centred = proj - mean
+        var = jnp.mean(centred * centred, axis=-1, keepdims=True)
+        gains = jnp.concatenate([gain_v[i : i + 1, :] for i in range(D // 128)], axis=1)
+        normed_v[step] = (centred * lax.rsqrt(var + 1e-05) * gains).astype(BF)
+
+    def fill(step, turn):
+        place = place_at(step)
+        normed = normed_v[step]
+        columns = [
+            jnp.dot(normed, w_qkv_v[:, kind * D + group * 256 : kind * D + group * 256 + 256], preferred_element_type=F32)
+            for kind, group in NEEDS[turn]
+        ]
+        lines = (dest_v[...] & (ROWS - 1)).astype(F32)
+        lines = jnp.broadcast_to(lines.reshape(8, 1, 128), (8, 32, 128)).reshape(CHUNK, 128)
+        r = iota((CHUNK, 128), 0)
+        wanted = ((r >> 3) & 3) * 32 + place * 8 + (r & 7)
+        position = jnp.sum(jnp.where(iota((CHUNK, 128), 1) == wanted, lines, 0.0), axis=1, keepdims=True).astype(I32)
+        for index, block in enumerate(pick_columns(turn, columns, position)):
+            lanes = pl.ds(index * 128, 128)
+            leaving[turn][:, place, :, lanes] = block.reshape(CHUNK // BLOCK, BLOCK, 128).astype(BF)
+
+    def leave(step, turn):
+        place = place_at(step)
+
+        @pl.loop(0, CHUNK // BLOCK)
+        def _(i):
+            to_slide = lax.rem(slide + i, SLIDES)
+            to_across = lax.rem(across + i // SLIDES, 4)
+
+            @pl.when((to_slide != slide) | (to_across != across) | (place != place_me))
+            def _():
+                pltpu.make_async_remote_copy(
+                    src_ref=leaving[turn].at[to_slide * 4 + to_across, place],
+                    dst_ref=coming[turn].at[me],
+                    send_sem=go_sem.at[turn],
+                    recv_sem=come_sem.at[turn],
+                    device_id=(to_slide, to_across * PLACES + place),
+                    device_id_type=MESH,
+                ).start()
+
+    def stay(turn):
+        copy = pltpu.make_async_copy(
+            leaving[turn].at[slide * 4 + across, place_me], coming[turn].at[me], stay_sem.at[turn]
+        )
+        copy.start()
+        copy.wait()
+
+    others = pl.ds(0, DEVICES - 1)
+
+    def arrived(turn):
+        part = coming[turn].at[others]
+        pltpu.make_async_copy(part, part, come_sem.at[turn]).wait()
+
+    def left(turn):
+        part = coming[turn].at[others]
+        pltpu.make_async_copy(part, part, go_sem.at[turn]).wait()
 
     def slot(d):
         return 2 * lax.rem(row + d // 2, 2) + lax.rem(col + d % 2, 2)
@@ -220,37 +195,38 @@
 
     sibling = (slide, seq + 1 - 2 * core)
     cross = (slide, (1 - half) * 8 + cross_slot(0) * 2 + core)
-    partners = [device(1), device(2), device(3), sibling, cross]
-
-    barrier = pltpu.get_barrier_semaphore()
-    for other in partners:
-        pl.semaphore_signal(barrier, inc=1, device_id=other, device_id_type=MESH)
-
-    rows_in = recv[...]
-    lane8 = iota((8, 128), 1)
-    weigh = jnp.where(lane8 == 64, 128.0, jnp.where(lane8 == 65, 1.0, 0.0)).astype(BF)
-    at = lax.dot_general(weigh, rows_in[:, 128:256], (((1,), (1,)), ((), ())), preferred_element_type=F32)
-    at = at[0:1].astype(I32)
+
     low64 = iota((64, 128), 1) < 64
 
-    def sort_class(cls, ref):
-        hit = (at - cls * 256) == iota((256, ROWS), 0)
-        one_hot = jnp.where(hit, 1.0, 0.0).astype(BF)
-        found = jnp.dot(one_hot, rows_in, preferred_element_type=F32)
+    def target(d):
+        return own.at[0] if d == 0 else stage.at[d - 1]
+
+    def mark():
+        lane8 = iota((8, 128), 1)
+        weigh = jnp.where(lane8 == 64, 128.0, jnp.where(lane8 == 65, 1.0, 0.0)).astype(BF)
+        ids = in0[...].reshape(ROWS, WIDTHS[0])[:, 128:256]
+        at = lax.dot_general(weigh, ids, (((1,), (1,)), ((), ())), preferred_element_type=F32)
+        at = at[0:1].astype(I32)
+        for d in range(4):
+            hit = (at - cls_of(d) * 256) == iota((256, ROWS), 0)
+            hot[d] = jnp.where(hit, 1.0, 0.0).astype(BF)
+
+    def sort(d, turn):
+        rows_in = coming[turn][...].reshape(ROWS, WIDTHS[turn])
+        found = jnp.dot(hot[d], rows_in, preferred_element_type=F32)
+        ref = target(d)
 
         def tile(a, t):
             return found[a * 64 : a * 64 + 64, t * 128 : t * 128 + 128]
 
-        for group in range(3):
-            for i in range(4):
-                ref[6 * group + i] = tile((2 * (group % 2) + i) % 4, KV_AT[group]).astype(BF)
-            for pair in range(2):
-                even, odd = tile(2 * pair, group // 2), tile(2 * pair + 1, group // 2)
-                if group == 1:
-                    even = pltpu.roll(even, 64, 1)
-                else:
-                    odd = pltpu.roll(odd, 64, 1)
-                ref[6 * group + 4 + pair] = jnp.where(low64, even, odd).astype(BF)
+        for i in range(4):
+            ref[6 * turn + i] = tile((2 * (turn % 2) + i) % 4, 0).astype(BF)
+        for pair in range(2):
+            if turn < 2:
+                even, odd = tile(2 * pair, 1), tile(2 * pair + 1, 1)
+                ref[6 * turn + 4 + pair] = jnp.where(low64, even, pltpu.roll(odd, 64, 1)).astype(BF)
+            if turn == 1:
+                ref[16 + pair] = jnp.where(low64, pltpu.roll(even, 64, 1), odd).astype(BF)
 
     def remote(src, dst, send, recv_, to):
         return pltpu.make_async_remote_copy(
@@ -266,16 +242,6 @@
         )
         copy.start()
         sends[d, group] = copy
-
-    for order, d in enumerate(ARRIVAL[1:]):
-        sort_class(cls_of(d), stage.at[d - 1])
-        if order == 0:
-            pl.semaphore_wait(barrier, len(partners))
-        send(d, 0)
-    for group in range(1, 3):
-        for d in ARRIVAL[1:]:
-            send(d, group)
-    sort_class(cls_of(0), own.at[0])
 
     sib_copies, x_copies, xs_copies = {}, {}, {}
 
@@ -397,11 +363,39 @@
         for e in (3, 1, 2, 0):
             give(e, group)
 
-    for group in range(3):
-        share(0, group)
+    def exchange(turn):
+        stay(turn)
+        arrived(turn)
+        if turn == 0:
+            mark()
+        for d in ARRIVAL[1:]:
+            sort(d, turn)
+            send(d, turn)
+        sort(0, turn)
+        share(0, turn)
+
+    for step in range(PLACES):
+        project(step)
+        if step == 0:
+            loads[1].wait()
+            loads[2].wait()
+        fill(step, 0)
+        if step == 0:
+            pl.semaphore_wait(barrier, DEVICES - 1)
+        leave(step, 0)
+    for step in range(PLACES):
+        fill(step, 1)
+        leave(step, 1)
+    for step in range(PLACES):
+        fill(step, 2)
+    exchange(0)
+    for step in range(PLACES):
+        leave(step, 2)
+    exchange(1)
     for d in ARRIVAL[1:]:
         share(d, 0)
     attend_half(0)
+    exchange(2)
     for d in ARRIVAL[1:]:
         share(d, 1)
     for d in ARRIVAL:
@@ -420,6 +414,7 @@
     for copy in outs:
         copy.wait()
     for group in range(3):
+        left(group)
         for d in range(4):
             if d > 0:
                 sends[d, group].wait_send()
@@ -428,15 +423,25 @@
             xs_copies[d, group].wait_send()
 
 
-def attend(recv, valid):
-    vmem = pl.BlockSpec(memory_space=pltpu.VMEM)
+def layer(tiles, dest, w_in, gain, w_qkv, valid):
+    hbm = pl.BlockSpec(memory_space=pltpu.HBM)
     dma = pltpu.SemaphoreType.DMA
+    blocks = DEVICES // PLACES
     return pl.pallas_call(
-        attend_kernel,
+        layer_kernel,
         out_shape=jax.ShapeDtypeStruct((4, 6, 64, 128), BF),
-        in_specs=[vmem, pl.BlockSpec(memory_space=pltpu.SMEM)],
-        out_specs=pl.BlockSpec(memory_space=pltpu.HBM),
+        in_specs=[hbm] * 5 + [pl.BlockSpec(memory_space=pltpu.SMEM)],
+        out_specs=hbm,
         scratch_shapes=[
+            pltpu.VMEM((PLACES, blocks, BLOCK, E), BF),
+            pltpu.VMEM((E, D), BF),
+            pltpu.VMEM((D, 3 * D), BF),
+            pltpu.VMEM((8, 128), I32),
+            pltpu.VMEM((D // 128, 128), F32),
+            pltpu.VMEM((PLACES, CHUNK, D), BF),
+            *[pltpu.VMEM((blocks, PLACES, BLOCK, width), BF) for width in WIDTHS],
+            *[pltpu.VMEM((DEVICES, BLOCK, width), BF) for width in WIDTHS],
+            pltpu.VMEM((4, 256, ROWS), BF),
             pltpu.VMEM((4, 18, 64, 128), BF),
             pltpu.VMEM((4, 12, 64, 128), BF),
             pltpu.VMEM((4, 6, 64, 128), BF),
@@ -453,21 +458,20 @@
             pltpu.VMEM((2, 128, 128), BF),
             pltpu.VMEM((3, 128, 128), BF),
             pltpu.VMEM((3, 128, 128), BF),
+            dma((4 + PLACES,)),
+            dma((3,)),
+            dma((3,)),
+            dma((3,)),
             dma((3, 3)),
             dma((3, 3)),
-            dma((4, 3)),
-            dma((4, 3)),
-            dma((4, 3)),
-            dma((4, 3)),
-            dma((4, 3)),
-            dma((4, 3)),
+            *[dma((4, 3)) for _ in range(6)],
             dma((3, 3)),
             dma((3, 3)),
             dma((3,)),
         ],
-        compiler_params=pltpu.CompilerParams(collective_id=1, has_side_effects=True, vmem_limit_bytes=VMEM_LIMIT),
-        name="attend",
-    )(recv, valid)
+        compiler_params=pltpu.CompilerParams(collective_id=0, has_side_effects=True, vmem_limit_bytes=VMEM_LIMIT),
+        name="layer",
+    )(tiles, dest, w_in, gain, w_qkv, valid)
 
 
 def output_kernel(rows_hbm, weight_hbm, out, rows_in, weight, spread, packed, load_sem, out_sem):
@@ -527,8 +531,15 @@
 
 
 def local(tiles, destination, valid_len, in_weight, norm_gain, qkv_weight, out_weight):
-    recv = project(tiles.reshape(SLIDES, 2, 2, PLACES, BLOCK, E), destination.reshape(8, 128), in_weight, norm_gain.reshape(D // 128, 128), qkv_weight)
-    back = attend(recv.reshape(ROWS, WIDE), valid_len)
+    blocks = DEVICES // PLACES
+    back = layer(
+        tiles.reshape(blocks, PLACES, BLOCK, E),
+        destination.reshape(8, 128),
+        in_weight,
+        norm_gain.reshape(D // 128, 128),
+        qkv_weight,
+        valid_len,
+    )
     return output(back, out_weight).reshape(1, ROWS, D)
 
 

time: 67.2 us -> 65.4 us (0.973)
  Pallas kernels: 66.8 us -> 65.1 us
    pallas_call x2 -> x1, Pallas kernels: 62.3 us -> 60.6 us  [layer(): pl.pallas_call(layer_kernel, out_shape=jax.ShapeDtypeStruct((4, 6, 64, 12...]
where the time goes in v5:
time: 65.4 us; the launch traced here: 65.3 us
  Pallas kernels  65.1 us (100%)
    pallas_call x1, Pallas kernels, layer(): pl.pallas_call(layer_kernel, out_shape=jax.ShapeDtypeStruct((4, 6, 64, 12...  60.6 us
    pallas_call x1, Pallas kernels, output(): pl.pallas_call(output_kernel, out_shape=jax.ShapeDtypeStruct((ROWS, D), B...  4.54 us

profile of v5, /device:TPU:1, one launch (start us, length us, event | category | flops | bytes accessed | tf_op | source)
XLA Modules:
  0.0 65.3 jit_solution(133419568839993110)
XLA Ops:
  0.0 60.6 %layer.1.rows_hbm = bf16[4,6,64,128]{3,2,1,0:T(8,128)(2,1)} custom-call(bf16[32,4,8,1536]{3,2,1,0:T(8,128)(2,1)} %bitcast.4, s32[8,128]{1,0:T(8,128)} %bitcast.5, bf16[1536,768]{1,0:T(8,128)(2,1)} %w_in.1, f32[6,128]{1,0:T(8,128)} %bitcast.6, bf16[768,2304]{1,0:T(8,128)(2,1)} %w_qkv.1, s32[8]{0:T(128)} %valid.1), custom_call_target="tpu_custom_call" | custom-call | tf_op jit(solution)/shard_map/layer/pallas_call | solution.py:430
  60.6 4.5 %output.1 = bf16[1024,768]{1,0:T(8,128)(2,1)} custom-call(bf16[4,6,64,128]{3,2,1,0:T(8,128)(2,1)} %layer.1.rows_hbm, bf16[768,768]{1,0:T(8,128)(2,1)} %weight_hbm.1), custom_call_target="tpu_custom_call" | custom-call | tf_op jit(solution)/shard_map/output/pallas_call | solution.py:515

commit v6 on v5

--- a/solution.py
+++ b/solution.py
@@ -27,8 +27,8 @@
     return lax.broadcasted_iota(I32, shape, dim)
 
 
-WIDTHS = (256, 256, 128)
-NEEDS = (((1, 0), (2, 0), (0, 0)), ((1, 1), (2, 1), (0, 1), (0, 2)), ((1, 2), (2, 2)))
+WIDTHS = (256, 384)
+NEEDS = (((1, 0), (2, 0), (0, 0)), ((1, 1), (2, 1), (0, 1), (0, 2), (1, 2), (2, 2)))
 
 
 def pick_columns(turn, columns, place):
@@ -53,6 +53,7 @@
         picked.append(jnp.where(low_lane, jnp.where(odd, pltpu.roll(q, 64, 1), q), ids))
     if turn == 1:
         picked.append(pair(heads[2] * 0.125, heads[3] * 0.125))
+        picked.append(pair(heads[4], heads[5]))
     return picked
 
 
@@ -79,7 +80,7 @@
 
 def layer_kernel(
     tiles, dest, w_in, gain, w_qkv, valid, back,
-    tiles_v, w_in_v, w_qkv_v, dest_v, gain_v, normed_v, out0, out1, out2, in0, in1, in2, hot,
+    tiles_v, w_in_v, w_qkv_v, dest_v, gain_v, normed_v, out0, out1, in0, in1, hot,
     own, sib, x_own, x_sib, stage, q_op, k_op, v_op, xk_op, xv_op, tops, sums, attn, q_tab, k_tab, x_tab,
     load_sem, go_sem, come_sem, stay_sem,
     send_sem, recv_sem, sib_send, sib_recv, x_send, x_recv, xs_send, xs_recv, out_send, out_recv, own_sem,
@@ -93,7 +94,7 @@
     row = lax.rem(seq // 4, 2)
     col = lax.rem(seq // 2, 2)
     core = lax.rem(seq, 2)
-    leaving, coming = (out0, out1, out2), (in0, in1, in2)
+    leaving, coming = (out0, out1), (in0, in1)
 
     def place_at(step):
         return lax.rem(place_me + step, PLACES)
@@ -117,10 +118,6 @@
         pl.semaphore_signal(barrier, inc=1, device_id=(other // SEQ, lax.rem(other, SEQ)), device_id_type=MESH)
 
     def project(step):
-        if step == 0:
-            loads[0].wait()
-            loads[3].wait()
-        loads[4 + step].wait()
         x = tiles_v[step].reshape(CHUNK, E)
         proj = jnp.dot(x, w_in_v[...], preferred_element_type=F32).astype(BF).astype(F32)
         mean = jnp.mean(proj, axis=-1, keepdims=True)
@@ -219,12 +216,12 @@
         def tile(a, t):
             return found[a * 64 : a * 64 + 64, t * 128 : t * 128 + 128]
 
-        for i in range(4):
-            ref[6 * turn + i] = tile((2 * (turn % 2) + i) % 4, 0).astype(BF)
+        for group, at_tile in ((0, 0),) if turn == 0 else ((1, 0), (2, 2)):
+            for i in range(4):
+                ref[6 * group + i] = tile((2 * (group % 2) + i) % 4, at_tile).astype(BF)
         for pair in range(2):
-            if turn < 2:
-                even, odd = tile(2 * pair, 1), tile(2 * pair + 1, 1)
-                ref[6 * turn + 4 + pair] = jnp.where(low64, even, pltpu.roll(odd, 64, 1)).astype(BF)
+            even, odd = tile(2 * pair, 1), tile(2 * pair + 1, 1)
+            ref[6 * turn + 4 + pair] = jnp.where(low64, even, pltpu.roll(odd, 64, 1)).astype(BF)
             if turn == 1:
                 ref[16 + pair] = jnp.where(low64, pltpu.roll(even, 64, 1), odd).astype(BF)
 
@@ -371,14 +368,22 @@
         for d in ARRIVAL[1:]:
             sort(d, turn)
             send(d, turn)
+        if turn == 1:
+            for d in ARRIVAL[1:]:
+                send(d, 2)
         sort(0, turn)
-        share(0, turn)
-
+        for group in (0,) if turn == 0 else (1, 2):
+            share(0, group)
+
+    for index in (0, 3, 4):
+        loads[index].wait()
+    project(0)
+    for index in (1, 2):
+        loads[index].wait()
     for step in range(PLACES):
-        project(step)
-        if step == 0:
-            loads[1].wait()
-            loads[2].wait()
+        if step + 1 < PLACES:
+            loads[5 + step].wait()
+            project(step + 1)
         fill(step, 0)
         if step == 0:
             pl.semaphore_wait(barrier, DEVICES - 1)
@@ -386,16 +391,11 @@
     for step in range(PLACES):
         fill(step, 1)
         leave(step, 1)
-    for step in range(PLACES):
-        fill(step, 2)
     exchange(0)
-    for step in range(PLACES):
-        leave(step, 2)
     exchange(1)
     for d in ARRIVAL[1:]:
         share(d, 0)
     attend_half(0)
-    exchange(2)
     for d in ARRIVAL[1:]:
         share(d, 1)
     for d in ARRIVAL:
@@ -406,15 +406,16 @@
     for d in ARRIVAL:
         share_cross(d, 1)
     attend_cross(0)
-    attend_half(2)
+    attend_cross(1)
     for d in ARRIVAL:
         share_cross(d, 2)
-    attend_cross(1)
+    attend_half(2)
     attend_cross(2)
     for copy in outs:
         copy.wait()
+    for turn in range(2):
+        left(turn)
     for group in range(3):
-        left(group)
         for d in range(4):
             if d > 0:
                 sends[d, group].wait_send()

time: 65.4 us -> 62.4 us (0.954)
  Pallas kernels: 65.1 us -> 62 us
    pallas_call x1, Pallas kernels: 60.6 us -> 57.5 us  [layer(): pl.pallas_call(layer_kernel, out_shape=jax.ShapeDtypeStruct((4, 6, 64, 12...]
where the time goes in v6:
time: 62.4 us; the launch traced here: 62.2 us
  Pallas kernels  62 us (99%)
    pallas_call x1, Pallas kernels, layer(): pl.pallas_call(layer_kernel, out_shape=jax.ShapeDtypeStruct((4, 6, 64, 12...  57.5 us
    pallas_call x1, Pallas kernels, output(): pl.pallas_call(output_kernel, out_shape=jax.ShapeDtypeStruct((ROWS, D), B...  4.54 us

profile of v6, /device:TPU:1, one launch (start us, length us, event | category | flops | bytes accessed | tf_op | source)
XLA Modules:
  0.0 62.2 jit_solution(7148408517609176259)
XLA Ops:
  0.0 57.5 %layer.1.rows_hbm = bf16[4,6,64,128]{3,2,1,0:T(8,128)(2,1)} custom-call(bf16[32,4,8,1536]{3,2,1,0:T(8,128)(2,1)} %bitcast.4, s32[8,128]{1,0:T(8,128)} %bitcast.5, bf16[1536,768]{1,0:T(8,128)(2,1)} %w_in.1, f32[6,128]{1,0:T(8,128)} %bitcast.6, bf16[768,2304]{1,0:T(8,128)(2,1)} %w_qkv.1, s32[8]{0:T(128)} %valid.1), custom_call_target="tpu_custom_call" | custom-call | tf_op jit(solution)/shard_map/layer/pallas_call | solution.py:431
  57.5 4.5 %output.1 = bf16[1024,768]{1,0:T(8,128)(2,1)} custom-call(bf16[4,6,64,128]{3,2,1,0:T(8,128)(2,1)} %layer.1.rows_hbm, bf16[768,768]{1,0:T(8,128)(2,1)} %weight_hbm.1), custom_call_target="tpu_custom_call" | custom-call | tf_op jit(solution)/shard_map/output/pallas_call | solution.py:516

commit v7 on v6

--- a/solution.py
+++ b/solution.py
@@ -145,21 +145,18 @@
     def leave(step, turn):
         place = place_at(step)
 
-        @pl.loop(0, CHUNK // BLOCK)
+        @pl.loop(1 if step == 0 else 0, CHUNK // BLOCK)
         def _(i):
             to_slide = lax.rem(slide + i, SLIDES)
             to_across = lax.rem(across + i // SLIDES, 4)
-
-            @pl.when((to_slide != slide) | (to_across != across) | (place != place_me))
-            def _():
-                pltpu.make_async_remote_copy(
-                    src_ref=leaving[turn].at[to_slide * 4 + to_across, place],
-                    dst_ref=coming[turn].at[me],
-                    send_sem=go_sem.at[turn],
-                    recv_sem=come_sem.at[turn],
-                    device_id=(to_slide, to_across * PLACES + place),
-                    device_id_type=MESH,
-                ).start()
+            pltpu.make_async_remote_copy(
+                src_ref=leaving[turn].at[to_slide * 4 + to_across, place],
+                dst_ref=coming[turn].at[me],
+                send_sem=go_sem.at[turn],
+                recv_sem=come_sem.at[turn],
+                device_id=(to_slide, to_across * PLACES + place),
+                device_id_type=MESH,
+            ).start()
 
     def stay(turn):
         copy = pltpu.make_async_copy(
@@ -326,19 +323,17 @@
 
     outs = []
 
-    def give(e, group):
+    def give(e, group, pair):
         d = ARRIVAL[e]
-        for pair in range(2):
-            acc = sums[group, e * 256 + pair * 128 : e * 256 + pair * 128 + 128, :]
-            position = steps + (start_of(half, slot(d), core) + 4 * pair)
-            out = jnp.where(position < length, acc / pltpu.roll(acc, 64, 1), 0.0)
-            attn[d, 2 * group + pair] = jnp.where(low64, pltpu.roll(out[0:64], 64, 1), out[64:128]).astype(BF)
-        part = pl.ds(2 * group, 2)
-        src, dst = attn.at[d, part], back.at[cls, part]
+        acc = sums[group, e * 256 + pair * 128 : e * 256 + pair * 128 + 128, :]
+        position = steps + (start_of(half, slot(d), core) + 4 * pair)
+        out = jnp.where(position < length, acc / pltpu.roll(acc, 64, 1), 0.0)
+        attn[d, 2 * group + pair] = jnp.where(low64, pltpu.roll(out[0:64], 64, 1), out[64:128]).astype(BF)
+        src, dst = attn.at[d, 2 * group + pair], back.at[cls, 2 * group + pair]
         if d > 0:
-            copy = remote(src, dst, out_send.at[group, d - 1], out_recv.at[group, d - 1], device(d))
+            copy = remote(src, dst, out_send.at[2 * group + pair, d - 1], out_recv.at[2 * group + pair, d - 1], device(d))
         else:
-            copy = pltpu.make_async_copy(src, dst, own_sem.at[group])
+            copy = pltpu.make_async_copy(src, dst, own_sem.at[2 * group + pair])
         copy.start()
         outs.append(copy)
 
@@ -347,18 +342,22 @@
             prepare(e, group)
         spans = [(begin, begin + 512) for begin in range(0, 2048, 512)]
         tops[group], sums[group] = mix(q_op[group], k_op, v_op, group, spans, None)
-
-    def attend_cross(group):
-        for e in range(4):
-            prepare_cross(e, group)
-        first = 128 * (group % 2)
-        rows = [pl.ds(e * 256 + first, 128) for e in range(4)]
-        q, top, acc = [jnp.concatenate([ref[group, r, :] for r in rows], axis=0) for ref in (q_op, tops, sums)]
-        _, acc = mix(q, xk_op, xv_op, group, ((0, 512), (512, 1024)), (top, acc))
-        for e in range(4):
-            sums[group, rows[e], :] = acc[e * 128 : e * 128 + 128]
         for e in (3, 1, 2, 0):
-            give(e, group)
+            give(e, group, 1 - group % 2)
+
+    def attend_cross(groups):
+        found = []
+        for group in groups:
+            first = 128 * (group % 2)
+            rows = [pl.ds(e * 256 + first, 128) for e in range(4)]
+            q, top, acc = [jnp.concatenate([ref[group, r, :] for r in rows], axis=0) for ref in (q_op, tops, sums)]
+            found.append((group, rows, mix(q, xk_op, xv_op, group, ((0, 512), (512, 1024)), (top, acc))[1]))
+        for group, rows, acc in found:
+            for e in range(4):
+                sums[group, rows[e], :] = acc[e * 128 : e * 128 + 128]
+        for group in groups:
+            for e in (3, 1, 2, 0):
+                give(e, group, group % 2)
 
     def exchange(turn):
         stay(turn)
@@ -405,12 +404,16 @@
         share(d, 2)
     for d in ARRIVAL:
         share_cross(d, 1)
-    attend_cross(0)
-    attend_cross(1)
+    for group in range(2):
+        for e in range(4):
+            prepare_cross(e, group)
+    attend_cross((0, 1))
     for d in ARRIVAL:
         share_cross(d, 2)
     attend_half(2)
-    attend_cross(2)
+    for e in range(4):
+        prepare_cross(e, 2)
+    attend_cross((2,))
     for copy in outs:
         copy.wait()
     for turn in range(2):
@@ -466,9 +469,9 @@
             dma((3, 3)),
             dma((3, 3)),
             *[dma((4, 3)) for _ in range(6)],
-            dma((3, 3)),
-            dma((3, 3)),
-            dma((3,)),
+            dma((6, 3)),
+            dma((6, 3)),
+            dma((6,)),
         ],
         compiler_params=pltpu.CompilerParams(collective_id=0, has_side_effects=True, vmem_limit_bytes=VMEM_LIMIT),
         name="layer",
@@ -476,35 +479,36 @@
 
 
 def output_kernel(rows_hbm, weight_hbm, out, rows_in, weight, spread, packed, load_sem, out_sem):
-    loads = [
-        pltpu.make_async_copy(weight_hbm, weight, load_sem.at[0]),
-        pltpu.make_async_copy(rows_hbm, rows_in, load_sem.at[1]),
-    ]
+    loads = [pltpu.make_async_copy(rows_hbm, rows_in, load_sem.at[0])]
+    for part in range(2):
+        lanes = pl.ds(part * (D // 2), D // 2)
+        loads.append(pltpu.make_async_copy(weight_hbm.at[:, lanes], weight.at[part], load_sem.at[1 + part]))
     for copy in loads:
         copy.start()
-    for copy in loads:
-        copy.wait()
+    loads[0].wait()
     low = iota((64, 128), 1) < 64
+    rows = []
     for cls in range(4):
-        heads = [weight[(cls + 4 * g) * 64 : (cls + 4 * g + 1) * 64, :] for g in range(3)]
-        wide = jnp.concatenate([w for w in heads for _ in range(2)], axis=0)
         columns = []
         for g in range(3):
             tiles = [rows_in[cls, 2 * g + a // 2] for a in range(4)]
             masked = [jnp.where(low == (a % 2 == 0), tile, jnp.zeros_like(tile)) for a, tile in enumerate(tiles)]
             columns.append(jnp.concatenate(masked, axis=0))
-        rows = jnp.concatenate(columns, axis=1)
-        total = jnp.dot(rows, wide, preferred_element_type=F32)
-        for a in range(4):
-            residue = cls + (a % 2) * 8 + (a // 2) * 4
-            for t in range(D // 128):
-                spread[t, pl.ds(residue, 64, stride=16), :] = total[a * 64 : a * 64 + 64, t * 128 : t * 128 + 128]
+        rows.append(jnp.concatenate(columns, axis=1))
     copies = []
-    for index in range(4):
-        span = pl.ds(index * 256, 256)
-        for t in range(D // 128):
-            packed[span, t * 128 : t * 128 + 128] = spread[t, span, :].astype(BF)
-        copy = pltpu.make_async_copy(packed.at[span], out.at[span], out_sem.at[index])
+    for part in range(2):
+        loads[1 + part].wait()
+        for cls in range(4):
+            heads = [weight[part, (cls + 4 * g) * 64 : (cls + 4 * g + 1) * 64, :] for g in range(3)]
+            wide = jnp.concatenate([w for w in heads for _ in range(2)], axis=0)
+            total = jnp.dot(rows[cls], wide, preferred_element_type=F32)
+            for a in range(4):
+                residue = cls + (a % 2) * 8 + (a // 2) * 4
+                for t in range(3):
+                    spread[3 * part + t, pl.ds(residue, 64, stride=16), :] = total[a * 64 : a * 64 + 64, t * 128 : t * 128 + 128]
+        for t in range(3):
+            packed[part, :, t * 128 : t * 128 + 128] = spread[3 * part + t].astype(BF)
+        copy = pltpu.make_async_copy(packed.at[part], out.at[:, pl.ds(part * (D // 2), D // 2)], out_sem.at[part])
         copy.start()
         copies.append(copy)
     for copy in copies:
@@ -520,11 +524,11 @@
         out_specs=hbm,
         scratch_shapes=[
             pltpu.VMEM((4, 6, 64, 128), BF),
-            pltpu.VMEM((D, D), BF),
+            pltpu.VMEM((2, D, D // 2), BF),
             pltpu.VMEM((D // 128, ROWS, 128), F32),
-            pltpu.VMEM((ROWS, D), BF),
+            pltpu.VMEM((2, ROWS, D // 2), BF),
+            pltpu.SemaphoreType.DMA((3,)),
             pltpu.SemaphoreType.DMA((2,)),
-            pltpu.SemaphoreType.DMA((4,)),
         ],
         compiler_params=pltpu.CompilerParams(vmem_limit_bytes=VMEM_LIMIT),
         name="output",

time: 62.4 us -> 61.1 us (0.979)
  Pallas kernels: 62 us -> 60.8 us
    pallas_call x1, Pallas kernels: 57.5 us -> 56.5 us  [layer(): pl.pallas_call(layer_kernel, out_shape=jax.ShapeDtypeStruct((4, 6, 64, 12...]
where the time goes in v7:
time: 61.1 us; the launch traced here: 61 us
  Pallas kernels  60.8 us (100%)
    pallas_call x1, Pallas kernels, layer(): pl.pallas_call(layer_kernel, out_shape=jax.ShapeDtypeStruct((4, 6, 64, 12...  56.5 us
    pallas_call x1, Pallas kernels, output(): pl.pallas_call(output_kernel, out_shape=jax.ShapeDtypeStruct((ROWS, D), B...  4.3 us

profile of v7, /device:TPU:1, one launch (start us, length us, event | category | flops | bytes accessed | tf_op | source)
XLA Modules:
  0.0 61.0 jit_solution(11754129649510374308)
XLA Ops:
  0.0 56.5 %layer.1.rows_hbm = bf16[4,6,64,128]{3,2,1,0:T(8,128)(2,1)} custom-call(bf16[32,4,8,1536]{3,2,1,0:T(8,128)(2,1)} %bitcast.4, s32[8,128]{1,0:T(8,128)} %bitcast.5, bf16[1536,768]{1,0:T(8,128)(2,1)} %w_in.1, f32[6,128]{1,0:T(8,128)} %bitcast.6, bf16[768,2304]{1,0:T(8,128)(2,1)} %w_qkv.1, s32[8]{0:T(128)} %valid.1), custom_call_target="tpu_custom_call" | custom-call | tf_op jit(solution)/shard_map/layer/pallas_call | solution.py:434
  56.5 4.3 %output.1 = bf16[1024,768]{1,0:T(8,128)(2,1)} custom-call(bf16[4,6,64,128]{3,2,1,0:T(8,128)(2,1)} %layer.1.rows_hbm, bf16[768,768]{1,0:T(8,128)(2,1)} %weight_hbm.1), custom_call_target="tpu_custom_call" | custom-call | tf_op jit(solution)/shard_map/output/pallas_call | solution.py:520

commit v8 on v7

--- a/solution.py
+++ b/solution.py
@@ -384,9 +384,11 @@
             loads[5 + step].wait()
             project(step + 1)
         fill(step, 0)
-        if step == 0:
+        if step == 1:
             pl.semaphore_wait(barrier, DEVICES - 1)
-        leave(step, 0)
+            leave(0, 0)
+        if step >= 1:
+            leave(step, 0)
     for step in range(PLACES):
         fill(step, 1)
         leave(step, 1)

time: 61.1 us -> 60.4 us (0.989)
  Pallas kernels: 60.8 us -> 59.9 us
    pallas_call x1, Pallas kernels: 56.5 us -> 55.6 us  [layer(): pl.pallas_call(layer_kernel, out_shape=jax.ShapeDtypeStruct((4, 6, 64, 12...]
where the time goes in v8:
time: 60.4 us; the launch traced here: 60.1 us
  Pallas kernels  59.9 us (99%)
    pallas_call x1, Pallas kernels, layer(): pl.pallas_call(layer_kernel, out_shape=jax.ShapeDtypeStruct((4, 6, 64, 12...  55.6 us
    pallas_call x1, Pallas kernels, output(): pl.pallas_call(output_kernel, out_shape=jax.ShapeDtypeStruct((ROWS, D), B...  4.3 us

profile of v8, /device:TPU:1, one launch (start us, length us, event | category | flops | bytes accessed | tf_op | source)
XLA Modules:
  0.0 60.1 jit_solution(7867312843148423661)
XLA Ops:
  0.0 55.6 %layer.1.rows_hbm = bf16[4,6,64,128]{3,2,1,0:T(8,128)(2,1)} custom-call(bf16[32,4,8,1536]{3,2,1,0:T(8,128)(2,1)} %bitcast.4, s32[8,128]{1,0:T(8,128)} %bitcast.5, bf16[1536,768]{1,0:T(8,128)(2,1)} %w_in.1, f32[6,128]{1,0:T(8,128)} %bitcast.6, bf16[768,2304]{1,0:T(8,128)(2,1)} %w_qkv.1, s32[8]{0:T(128)} %valid.1), custom_call_target="tpu_custom_call" | custom-call | tf_op jit(solution)/shard_map/layer/pallas_call | solution.py:436
  55.6 4.3 %output.1 = bf16[1024,768]{1,0:T(8,128)(2,1)} custom-call(bf16[4,6,64,128]{3,2,1,0:T(8,128)(2,1)} %layer.1.rows_hbm, bf16[768,768]{1,0:T(8,128)(2,1)} %weight_hbm.1), custom_call_target="tpu_custom_call" | custom-call | tf_op jit(solution)/shard_map/output/pallas_call | solution.py:522
